TPU v7x, 32 devices: a whole 2x2x4 slice. The times are simulated.
32 devices in a mesh: dp: 16 (over z, y, x), tensor: 2 (over core).
Axes of the slice: x: 2, y: 2, z: 4, core: 2. Of those that a mesh axis runs over, the one named last changes fastest.
Arguments:
- inputs: bfloat16 [8192, 768], P(('dp', 'tensor')), may hold values from -8 to 8
- segments: int32 [16, 512], P('dp'), may hold values from 0 to 3, as said below
- norm_gains: float32 [2, 768], replicated, may hold values from 0.1 to 1.9
- norm_shifts: float32 [2, 768], replicated, may hold values from -3 to 3
- qkv_weight: bfloat16 [3, 768, 768], P(None, 'dp', 'tensor'), may hold values from -2 to 2
- qkv_bias: float32 [2, 768], P(None, 'tensor'), may hold values from -3 to 3
- out_weight: bfloat16 [768, 768], P('tensor', 'dp'), may hold values from -1.75 to 1.75
- out_biases: float32 [2, 768], replicated, may hold values from -3 to 3
- up_weight: bfloat16 [768, 3072], P('dp', 'tensor'), may hold values from -0.21875 to 0.21875
- up_bias: float32 [3072], P('tensor'), may hold values from -3 to 3
- down_weight: bfloat16 [3072, 768], P('tensor', 'dp'), may hold values from -0.109375 to 0.109375
- cotangent: bfloat16 [8192, 768], P(('dp', 'tensor')), may hold values from -6 to 6
Outputs:
- output: bfloat16 [8192, 768], P(('dp', 'tensor'))
- input_grad: float32 [8192, 768], P(('dp', 'tensor'))
- norm_gains_grad: float32 [2, 768], replicated
- norm_shifts_grad: float32 [2, 768], replicated
- qkv_weight_grad: float32 [3, 768, 768], P(None, 'dp', 'tensor')
- qkv_bias_grad: float32 [2, 768], P(None, 'tensor')
- out_weight_grad: float32 [768, 768], P('tensor', 'dp')
- out_biases_grad: float32 [2, 768], replicated
- up_weight_grad: float32 [768, 3072], P('dp', 'tensor')
- up_bias_grad: float32 [3072], P('tensor')
- down_weight_grad: float32 [3072, 768], P('tensor', 'dp')
Inputs may be any that keep to these rules, and one draw needn't show every extreme that they name: `segments`: within each sequence of 512 tokens the segment numbers start at 0 and never fall; each rise marks the start of another document.
All inputs are finite; a program needn't handle non-finite values.
Results may differ from a plain program's by a relative error of at most 0.012.
The roundings to bfloat16 on the way count: a program that leaves them out, or rounds other values in their place, can miss the bound.
Values may be sent and summed in bfloat16 or wider, within the bound.
A program may use at most 128 MiB of HBM per device.

v0:
```python
import jax
import jax.numpy as jnp
from jax import lax
from jax.experimental import pallas as pl
from jax.experimental.pallas import tpu as pltpu
from jax.sharding import PartitionSpec as P

HEAD = 64


EPSILON = 1e-05
MASKED = -1e30


def normalize(row_block, gain, shift):
    center = jnp.mean(row_block, axis=-1, keepdims=True)
    centered = row_block - center
    spread = jnp.mean(centered * centered, axis=-1, keepdims=True)
    inverse = lax.rsqrt(spread + EPSILON)
    unit_rows = centered * inverse
    return (unit_rows * gain + shift, unit_rows, inverse)


def normalize_back(grad_rows, unit_rows, inverse, gain):
    scaled = grad_rows * gain
    first_mean = jnp.mean(scaled, axis=-1, keepdims=True)
    second_mean = jnp.mean(scaled * unit_rows, axis=-1, keepdims=True)
    return inverse * (scaled - first_mean - unit_rows * second_mean)


def gaussian_unit(values_in):
    return jax.nn.gelu(values_in, approximate=True)


def dot(left, right, left_dim, right_dim):
    return lax.dot_general(
        left, right, (((left_dim,), (right_dim,)), ((), ())), preferred_element_type=jnp.float32
    )


def allowed_block(seg_column, seg_row, start, rows, span):
    row_at = lax.broadcasted_iota(jnp.int32, (rows, span), 0) + start
    col_at = lax.broadcasted_iota(jnp.int32, (rows, span), 1)
    same = seg_column[start : start + rows, :] == seg_row[:, :span]
    return same & (row_at >= col_at)


def attend_kernel(stack_ref, seg_column_ref, seg_row_ref, mixed_ref, log_ref):
    length, width = mixed_ref.shape
    heads = width // HEAD
    rows = length // 2
    seg_column, seg_row = seg_column_ref[...], seg_row_ref[0]
    for block in range(2):
        start, span = block * rows, (block + 1) * rows
        allowed = allowed_block(seg_column, seg_row, start, rows, span)
        for head in range(heads):
            at = head * HEAD
            queries = stack_ref[start:span, at : at + HEAD]
            keys_in = stack_ref[:span, width + at : width + at + HEAD]
            values_in = stack_ref[:span, 2 * width + at : 2 * width + at + HEAD]
            scores = jnp.where(allowed, dot(queries, keys_in, 1, 1) * HEAD ** (-0.5), MASKED)
            top = jnp.max(scores, axis=-1, keepdims=True)
            total = jnp.sum(jnp.exp(scores - top), axis=-1, keepdims=True)
            log_total = top + jnp.log(total)
            soft = jnp.exp(scores - log_total).astype(jnp.bfloat16)
            mixed_ref[start:span, at : at + HEAD] = dot(soft, values_in, 1, 0).astype(jnp.bfloat16)
            log_ref[start:span, head : head + 1] = log_total


def attend_back_kernel(
    stack_ref, seg_column_ref, seg_row_ref, log_ref, grad_ref, low_ref, sums_ref
):
    length, width = grad_ref.shape
    heads = width // HEAD
    rows = length // 2
    seg_column, seg_row = seg_column_ref[...], seg_row_ref[0]
    masks = [
        allowed_block(seg_column, seg_row, block * rows, rows, (block + 1) * rows)
        for block in range(2)
    ]
    sums_ref[0] = jnp.zeros(sums_ref.shape[1:], jnp.float32)
    for head in range(heads):
        at = head * HEAD
        grad_keys, grad_values, query_sum = [], [], 0.0
        for block in range(2):
            start, span = block * rows, (block + 1) * rows
            queries = stack_ref[start:span, at : at + HEAD]
            keys_in = stack_ref[:span, width + at : width + at + HEAD]
            values_in = stack_ref[:span, 2 * width + at : 2 * width + at + HEAD]
            grad_mixed = grad_ref[start:span, at : at + HEAD]
            scores = jnp.where(masks[block], dot(queries, keys_in, 1, 1) * HEAD ** (-0.5), MASKED)
            probs = jnp.exp(scores - log_ref[start:span, head : head + 1])
            soft = probs.astype(jnp.bfloat16)
            grad_probs = dot(grad_mixed, values_in, 1, 1)
            row_dot = jnp.sum(probs * grad_probs, axis=-1, keepdims=True)
            grad_scores = (probs * (grad_probs - row_dot) * HEAD ** (-0.5)).astype(jnp.bfloat16)
            grad_queries = dot(grad_scores, keys_in, 1, 0)
            low_ref[start:span, at : at + HEAD] = grad_queries.astype(jnp.bfloat16)
            query_sum = query_sum + jnp.sum(grad_queries, axis=0, keepdims=True)
            grad_keys.append(dot(grad_scores, queries, 0, 0))
            grad_values.append(dot(soft, grad_mixed, 0, 0))
        sums_ref[0, 0:1, at : at + HEAD] = query_sum
        value_sum = 0.0
        for slot, pair in ((1, grad_keys), (2, grad_values)):
            where = slot * width + at
            upper = pair[0] + pair[1][:rows]
            lower = pair[1][rows:]
            low_ref[:rows, where : where + HEAD] = upper.astype(jnp.bfloat16)
            low_ref[rows:, where : where + HEAD] = lower.astype(jnp.bfloat16)
            if slot == 2:
                value_sum = jnp.sum(upper, axis=0, keepdims=True)
                value_sum = value_sum + jnp.sum(lower, axis=0, keepdims=True)
        sums_ref[0, 1:2, at : at + HEAD] = value_sum


def row_spec(length, width):
    return pl.BlockSpec((length, width), lambda at: (at, 0))


def attend(stack, seg_column, segments, width):
    seqs, length = segments.shape
    heads = width // HEAD
    return pl.pallas_call(
        attend_kernel,
        grid=(seqs,),
        in_specs=[
            row_spec(length, 3 * width),
            row_spec(length, 1),
            pl.BlockSpec((1, 1, length), lambda at: (at, 0, 0)),
        ],
        out_specs=[row_spec(length, width), row_spec(length, heads)],
        out_shape=[
            jax.ShapeDtypeStruct((seqs * length, width), jnp.bfloat16),
            jax.ShapeDtypeStruct((seqs * length, heads), jnp.float32),
        ],
        compiler_params=pltpu.CompilerParams(vmem_limit_bytes=40 * 2**20),
        cost_estimate=pl.CostEstimate(
            flops=8 * seqs * length * length * width, bytes_accessed=10**7, transcendentals=0
        ),
    )(stack, seg_column, segments[:, None, :])


def attend_back(stack, seg_column, segments, log_total, grad_mixed):
    seqs, length = segments.shape
    width = grad_mixed.shape[1]
    heads = width // HEAD
    low, sums = pl.pallas_call(
        attend_back_kernel,
        grid=(seqs,),
        in_specs=[
            row_spec(length, 3 * width),
            row_spec(length, 1),
            pl.BlockSpec((1, 1, length), lambda at: (at, 0, 0)),
            row_spec(length, heads),
            row_spec(length, width),
        ],
        out_specs=[
            row_spec(length, 3 * width),
            pl.BlockSpec((1, 8, width), lambda at: (at, 0, 0)),
        ],
        out_shape=[
            jax.ShapeDtypeStruct((seqs * length, 3 * width), jnp.bfloat16),
            jax.ShapeDtypeStruct((seqs, 8, width), jnp.float32),
        ],
        compiler_params=pltpu.CompilerParams(vmem_limit_bytes=40 * 2**20),
        cost_estimate=pl.CostEstimate(
            flops=20 * seqs * length * length * width, bytes_accessed=2 * 10**7, transcendentals=0
        ),
    )(stack, seg_column, segments[:, None, :], log_total, grad_mixed)
    return low, jnp.sum(sums, axis=0)[:2].reshape(-1)


def tie(*values):
    return lax.optimization_barrier(values)


class Gather:
    def __init__(self, shard, order, data_rank, data_count, bit_count):
        self.rows, self.cols = shard.shape
        self.order, self.count, self.bits = list(order), data_count, bit_count
        self.mine = [(data_rank >> (bit_count - 1 - place)) & 1 for place in range(bit_count)]
        self.done = []
        self.held = jnp.zeros(bit_shape(bit_count) + shard.shape, shard.dtype)
        self.piece = shard.reshape((1,) * bit_count + shard.shape)
        self.put(self.piece, self.mine)

    def put(self, piece, starts):
        zero = jnp.int32(0)
        self.held = lax.dynamic_update_slice(self.held, piece, list(starts) + [zero, zero])

    def step(self, steps=1):
        zero = jnp.int32(0)
        for _ in range(steps):
            bit = self.order.pop(0)
            place = self.bits - 1 - bit
            arrived = lax.ppermute(self.piece, "dp", partner_pairs(self.count, 1 << bit))
            target = [zero if at in self.done else self.mine[at] for at in range(self.bits)]
            target[place] = 1 - self.mine[place]
            self.put(arrived, target)
            self.done.append(place)
            if self.order:
                starts = [zero if at in self.done else self.mine[at] for at in range(self.bits)]
                sizes = [2 if at in self.done else 1 for at in range(self.bits)]
                self.piece = lax.dynamic_slice(
                    self.held, starts + [zero, zero], sizes + [self.rows, self.cols]
                )

    def whole(self):
        return self.held.reshape(self.count * self.rows, self.cols)


class Scatter:
    def __init__(self, term, order, data_rank, data_count, bit_count):
        self.rows, self.cols = term.shape[0] // data_count, term.shape[1]
        self.order, self.count, self.bits = list(order), data_count, bit_count
        self.mine = [(data_rank >> (bit_count - 1 - place)) & 1 for place in range(bit_count)]
        self.held = term.reshape(bit_shape(bit_count) + (self.rows, self.cols))

    def step(self, steps=1):
        for _ in range(steps):
            bit = self.order.pop(0)
            place = self.bits - 1 - bit
            away = lax.dynamic_slice_in_dim(self.held, 1 - self.mine[place], 1, place)
            kept = lax.dynamic_slice_in_dim(self.held, self.mine[place], 1, place)
            arrived = lax.ppermute(
                away.astype(jnp.bfloat16), "dp", partner_pairs(self.count, 1 << bit)
            )
            self.held = kept + arrived.astype(jnp.float32)

    def whole(self):
        self.step(len(self.order))
        return self.held.reshape(self.rows, self.cols)


def partner_pairs(count, step):
    return [(place, place ^ step) for place in range(count)]


def bit_shape(bit_count):
    return (2,) * bit_count


def total_over(flat, data_count, bit_count):
    for bit in range(bit_count):
        flat = flat + lax.ppermute(flat, "dp", partner_pairs(data_count, 1 << bit))
    return flat


def local(
    inputs,
    segments,
    norm_gains,
    norm_shifts,
    qkv_weight,
    qkv_bias,
    out_weight,
    out_biases,
    up_weight,
    up_bias,
    down_weight,
    cotangent,
):
    local_rows = inputs.shape[0]
    seq_count = segments.shape[0]
    seq_length = segments.shape[1]
    model_width = inputs.shape[1]
    tensor_rank = lax.axis_index("tensor")
    data_rank = lax.axis_index("dp")
    data_count = lax.axis_size("dp")
    bit_count = data_count.bit_length() - 1
    head_cols = qkv_weight.shape[2]
    hidden_cols = up_weight.shape[1]
    heads_here = head_cols // HEAD
    block_rows = seq_count * seq_length
    links = (data_rank, data_count, bit_count)
    rest = [bit for bit in range(bit_count - 1, 2, -1)]
    order_up = rest + [2, 1, 0]
    order_down = rest + [2, 0, 1]
    order_turn = rest + [1, 0, 2]
    orders = (order_turn, order_up, order_down)

    qkv_parts = [Gather(qkv_weight[at], orders[at], *links) for at in range(3)]
    out_part = Gather(out_weight.T, order_turn, *links)
    up_part = Gather(up_weight, order_up, *links)
    down_part = Gather(down_weight.T, order_down, *links)
    later = (out_part, up_part, down_part)
    early = bit_count - 2
    for part in qkv_parts:
        part.step(bit_count - 1)
    for part in later:
        part.step(early)
    tied = tie(*[part.piece for part in qkv_parts], *[part.piece for part in later])
    for at in range(3):
        qkv_parts[at].piece, later[at].piece = tied[at], tied[3 + at]
    for part in qkv_parts:
        part.step()
    for part in later:
        part.step()

    def spread(row_block):
        return lax.all_gather(row_block, "tensor", axis=0, tiled=True)

    def collect(left_rows, right_matrix, dims):
        def term(rank):
            part = lax.dynamic_slice_in_dim(left_rows, rank * local_rows, local_rows, 0)
            return lax.dot_general(
                part, right_matrix, (dims, ((), ())), preferred_element_type=jnp.float32
            )

        arrived = lax.ppermute(term(1 - tensor_rank), "tensor", [(0, 1), (1, 0)])
        return term(tensor_rank) + arrived

    plain, turned = ((1,), (0,)), ((1,), (1,))
    stream = inputs.astype(jnp.float32)
    normed, unit_one, inverse_one = normalize(stream, norm_gains[0], norm_shifts[0])
    hidden_one = spread(normed.astype(jnp.bfloat16))
    grad_stream = cotangent.astype(jnp.float32)
    grad_rows = spread(cotangent)
    zeros = jnp.zeros((head_cols,), jnp.float32)
    biases = (qkv_bias[0], zeros, qkv_bias[1])
    qkv_full = [part.whole() for part in qkv_parts]
    stack_rows = jnp.concatenate(
        [
            (
                jnp.dot(hidden_one, qkv_full[at], preferred_element_type=jnp.float32) + biases[at]
            ).astype(jnp.bfloat16)
            for at in range(3)
        ],
        axis=1,
    )
    tied = tie(stack_rows, *[part.piece for part in later])
    stack_rows = tied[0]
    for part, piece in zip(later, tied[1:]):
        part.piece = piece
        part.step()
    out_full, up_full, down_full = [part.whole() for part in later]
    seg_column = segments.reshape(block_rows, 1)
    mixed_rows, log_total = attend(stack_rows, seg_column, segments, head_cols)
    middle = stream + collect(mixed_rows, out_full, turned) + out_biases[0]
    normed_two, unit_two, inverse_two = normalize(middle, norm_gains[1], norm_shifts[1])
    hidden_two = spread(normed_two.astype(jnp.bfloat16))
    before = jnp.dot(hidden_two, up_full, preferred_element_type=jnp.float32) + up_bias
    activated = gaussian_unit(before).astype(jnp.bfloat16)
    down_turned = jnp.einsum("rd,rj->dj", grad_rows, activated, preferred_element_type=jnp.float32)
    down_sum = Scatter(down_turned, order_down[::-1], *links)
    down_sum.step()
    grad_active = jnp.dot(grad_rows, down_full, preferred_element_type=jnp.float32)
    grad_before = jax.vjp(gaussian_unit, before)[1](grad_active)[0]
    before_low = grad_before.astype(jnp.bfloat16)
    grad_up = jnp.einsum("rd,rj->dj", hidden_two, before_low, preferred_element_type=jnp.float32)
    up_sum = Scatter(grad_up, order_up[::-1], *links)
    up_sum.step()
    grad_hidden_two = collect(before_low, up_full, turned)
    grad_middle = grad_stream + normalize_back(
        grad_hidden_two, unit_two, inverse_two, norm_gains[1]
    )
    middle_rows = spread(grad_middle.astype(jnp.bfloat16))
    out_turned = jnp.einsum(
        "rd,rj->dj", middle_rows, mixed_rows, preferred_element_type=jnp.float32
    )
    out_sum = Scatter(out_turned, order_turn[::-1], *links)
    out_sum.step()
    grad_mixed = jnp.dot(middle_rows, out_full, preferred_element_type=jnp.float32).astype(
        jnp.bfloat16
    )
    grad_mixed, down_sum.held = tie(grad_mixed, down_sum.held)
    down_sum.step()
    result = (middle + collect(activated, down_full, turned) + out_biases[1]).astype(jnp.bfloat16)
    stack_low, bias_sums = attend_back(stack_rows, seg_column, segments, log_total, grad_mixed)
    stack_low, up_sum.held, out_sum.held = tie(stack_low, up_sum.held, out_sum.held)
    up_sum.step()
    out_sum.step()
    qkv_sums = []
    for at in range(3):
        term = dot(hidden_one, stack_low[:, at * head_cols : (at + 1) * head_cols], 0, 0)
        qkv_sums.append(Scatter(term, orders[at][::-1], *links))
        qkv_sums[at].step()
    grad_hidden_one = collect(stack_low, jnp.concatenate(qkv_full, axis=1), turned)
    grad_input = grad_middle + normalize_back(grad_hidden_one, unit_one, inverse_one, norm_gains[0])
    vectors = jnp.concatenate(
        [
            jnp.sum(grad_hidden_one * unit_one, axis=0),
            jnp.sum(grad_hidden_two * unit_two, axis=0),
            jnp.sum(grad_hidden_one, axis=0),
            jnp.sum(grad_hidden_two, axis=0),
            jnp.sum(grad_middle, axis=0),
            jnp.sum(grad_stream, axis=0),
        ]
    )
    vectors = vectors + lax.ppermute(vectors, "tensor", [(0, 1), (1, 0)])
    flat = jnp.concatenate(
        [
            vectors,
            bias_sums,
            jnp.sum(grad_before, axis=0),
        ]
    )
    flat = total_over(flat, data_count, bit_count)
    qkv_summed = jnp.stack([part.whole() for part in qkv_sums])
    out_summed, down_summed = out_sum.whole().T, down_sum.whole().T
    up_summed = up_sum.whole()
    vector_total = flat[: 6 * model_width].reshape(6, model_width)
    rest_total = flat[6 * model_width :]
    qkv_bias_grad = rest_total[: 2 * head_cols].reshape(2, head_cols)
    up_bias_grad = rest_total[2 * head_cols :]
    return (
        result,
        grad_input,
        vector_total[0:2],
        vector_total[2:4],
        qkv_summed,
        qkv_bias_grad,
        out_summed,
        vector_total[4:6],
        up_summed,
        up_bias_grad,
        down_summed,
    )


def solution(mesh):
    in_specs = (
        P(("dp", "tensor"), None),
        P("dp", None),
        P(),
        P(),
        P(None, "dp", "tensor"),
        P(None, "tensor"),
        P("tensor", "dp"),
        P(),
        P("dp", "tensor"),
        P("tensor"),
        P("tensor", "dp"),
        P(("dp", "tensor"), None),
    )
    out_specs = (
        P(("dp", "tensor"), None),
        P(("dp", "tensor"), None),
        P(),
        P(),
        P(None, "dp", "tensor"),
        P(None, "tensor"),
        P("tensor", "dp"),
        P(),
        P("dp", "tensor"),
        P("tensor"),
        P("tensor", "dp"),
    )
    return jax.shard_map(local, mesh=mesh, in_specs=in_specs, out_specs=out_specs, check_vma=False)
```

profile of v0, /device:TPU:0, one launch (start us, length us, event | category | flops | bytes accessed | tf_op | source)
XLA Modules:
  0.0 287.3 jit_solution(8185695873525606286)
XLA Ops:
  0.7 4.1 %collective-permute-start.9 = (bf16[1,1,1,1,48,384]{5,4,3,2,1,0:T(8,128)(2,1)}, bf16[1,1,1,1,48,384]{5,4,3,2,1,0:T(8,128)(2,1)}, u32[]{:S(2)}, u32[]{:S(2)}) collective-permute-start(bf16[1,1,1,1,48,384]{5,4,3,2,1,0:T(8,128)(2,1)} %bitcast.114), channel_id=1, source_target_pairs={{0,16},{2,18},{4,20},{6,22},{8,24},{10,26},{12,28},{14,30},{16,0},... | collective-permute-start | bytes 110600 | tf_op jit(solution)/shard_map/ppermute | solution.py:196
  6.2 2.9 %collective-permute-start = (bf16[1,1,1,1,48,384]{5,4,3,2,1,0:T(8,128)(2,1)S(1)}, bf16[1,1,1,1,48,384]{5,4,3,2,1,0:T(8,128)(2,1)}, u32[]{:S(2)}, u32[]{:S(2)}) collective-permute-start(bf16[1,1,1,1,48,384]{5,4,3,2,1,0:T(8,128)(2,1)S(1)} %get-tuple-element.71), channel_id=1, source_target_pairs={{0,16},{2,18},{4,20},{6,22},{8,24},{10,26},{12,28},{14,30},{16,0},... | collective-permute-start | bytes 110600 | tf_op jit(solution)/shard_map/ppermute | solution.py:196
  9.2 2.9 %collective-permute-start.13 = (bf16[1,1,1,1,48,1536]{5,4,3,2,1,0:T(8,128)(2,1)}, bf16[1,1,1,1,48,1536]{5,4,3,2,1,0:T(8,128)(2,1)}, u32[]{:S(2)}, u32[]{:S(2)}) collective-permute-start(bf16[1,1,1,1,48,1536]{5,4,3,2,1,0:T(8,128)(2,1)} %bitcast.113), channel_id=1, source_target_pairs={{0,16},{2,18},{4,20},{6,22},{8,24},{10,26},{12,28},{14,30},{16,0},... | collective-permute-start | bytes 442376 | tf_op jit(solution)/shard_map/ppermute | solution.py:196
  23.0 1.9 collective-permute-start.4
  40.6 1.9 collective-permute-start.14
  42.8 3.7 %collective-permute-done.12 = bf16[2,1,1,1,48,1536]{5,4,3,2,1,0:T(8,128)(2,1)S(1)} collective-permute-done((bf16[2,1,1,1,48,1536]{5,4,3,2,1,0:T(8,128)(2,1)S(1)}, bf16[2,1,1,1,48,1536]{5,4,3,2,1,0:T(8,128)(2,1)S(1)}, u32[]{:S(2)}, u32[]{:S(2)}) %collective-permute-start.12) | collective-permute-done | bytes 294944 | tf_op jit(solution)/shard_map/ppermute | solution.py:196
  53.1 2.4 all_gather.12
  57.3 1.8 collective-permute-start.17
  61.6 3.7 %collective-permute-done.16 = bf16[2,2,2,1,48,384]{5,4,3,2,1,0:T(8,128)(2,1)S(1)} collective-permute-done((bf16[2,2,2,1,48,384]{5,4,3,2,1,0:T(8,128)(2,1)S(1)}, bf16[2,2,2,1,48,384]{5,4,3,2,1,0:T(8,128)(2,1)S(1)}, u32[]{:S(2)}, u32[]{:S(2)}) %collective-permute-start.16) | collective-permute-done | bytes 294944 | tf_op jit(solution)/shard_map/ppermute | solution.py:196
  68.8 8.4 %collective-permute-done.20 = bf16[2,2,1,1,48,1536]{5,4,3,2,1,0:T(8,128)(2,1)S(1)} collective-permute-done((bf16[2,2,1,1,48,1536]{5,4,3,2,1,0:T(8,128)(2,1)S(1)}, bf16[2,2,1,1,48,1536]{5,4,3,2,1,0:T(8,128)(2,1)S(1)}, u32[]{:S(2)}, u32[]{:S(2)}) %collective-permute-start.20) | collective-permute-done | bytes 589856 | tf_op jit(solution)/shard_map/ppermute | solution.py:196
  78.0 2.4 constant_dynamic-slice_fusion
  81.2 2.4 constant_dynamic-slice_fusion.1
  85.0 5.6 %shard_map.203 = (bf16[512,384]{1,0:T(8,128)(2,1)S(1)}, f32[512,6]{1,0:T(8,128)S(1)}) custom-call(bf16[512,1152]{1,0:T(8,128)(2,1)S(1)} %pad_maximum_fusion.1.stack_ref, s32[512,1]{1,0:T(8,128)S(1)} %copy.29.seg_column_ref, s32[1,1,512]{2,1,0:T(1,128)S(1)} %bitcast.86), custom_call_target="tpu_custom_call" | custom-call | flops 805306368 | bytes 10000000 | tf_op jit(solution)/shard_map/pallas_call | solution.py:123
  94.5 3.0 %all_gather.14 = bf16[512,768]{1,0:T(8,128)(2,1)S(1)} all-gather(bf16[256,768]{1,0:T(8,128)(2,1)} %param.23), channel_id=1, replica_groups=mesh['dp'=16,'tensor'=2] {'tensor'}, dimensions={0}, use_global_device_ids=true | all-gather | bytes 1179648 | tf_op jit(solution)/shard_map/all_gather | solution.py:301
  98.1 1.8 collective-permute-start.24
  99.9 1.8 fusion.58
  102.2 2.4 all_gather.13
  104.5 21.3 %collective-permute-done.23 = bf16[2,2,2,1,48,1536]{5,4,3,2,1,0:T(8,128)(2,1)S(1)} collective-permute-done((bf16[2,2,2,1,48,1536]{5,4,3,2,1,0:T(8,128)(2,1)}, bf16[2,2,2,1,48,1536]{5,4,3,2,1,0:T(8,128)(2,1)S(1)}, u32[]{:S(2)}, u32[]{:S(2)}) %collective-permute-start.23) | collective-permute-done | bytes 1179680 | tf_op jit(solution)/shard_map/ppermute | solution.py:196
  127.0 3.6 %multiply_convert_fusion = (bf16[512,1536]{1,0:T(8,128)(2,1)S(1)}, f32[512,1536]{1,0:T(8,128)S(1)}) fusion(f32[1536]{0:T(1024)S(1)} %copy-done.39, bf16[512,768]{1,0:T(8,128)(2,1)S(1)} %all_gather.13, bf16[768,1536]{1,0:T(8,128)(2,1)} %bitcast.16), kind=kOutput, calls=%fused_computation.10 | convolution fusion | flops 1215823872 | bytes 7870464 | tf_op jit(solution)/shard_map/dot_general | solution.py:342
  131.7 4.6 %fusion.56 = (f32[1536]{0:T(1024)S(1)}, bf16[512,1536]{1,0:T(8,128)(2,1)S(1)}) fusion(f32[512,1536]{1,0:T(8,128)S(1)} %get-tuple-element.80, bf16[512,768]{1,0:T(8,128)(2,1)S(1)} %all_gather.14, bf16[768,1536]{1,0:T(8,128)(2,1)} %bitcast.17), kind=kOutput, calls=%fused_computation.205 | convolution fusion | flops 1224473088 | bytes 7870464 | tf_op jit(solution)/shard_map/dot_general | solution.py:347
  136.3 2.5 fusion.27
  140.2 2.5 fusion.30
  145.6 1.9 collective-permute-start.27
  147.5 3.3 %multiply_reduce_fusion = (f32[768]{0:T(1024)}, f32[256]{0:T(256)S(1)}, f32[256]{0:T(256)S(1)}, f32[768]{0:T(1024)}, f32[256,768]{1,0:T(8,128)S(1)}) fusion(f32[256,768]{1,0:T(8,128)S(1)} %get-tuple-element.78, f32[256]{0:T(256)S(1)} %add_rsqrt_fusion, f32[256]{0:T(256)S(1)} %broadcast_multiply_fusion.4, f32[768]{0:T(1024)S(1)} %get-tuple-element.85, ...), kind=kOutput, calls=%fused_computation.54 | convolution fusion | flops 605943808 | bytes 5519364 | tf_op jit(solution)/shard_map/dot_general | solution.py:306
  151.8 2.6 all_gather.15
  156.4 3.3 %fusion.12 = bf16[256,768]{1,0:T(8,128)(2,1)} fusion(f32[256,768]{1,0:T(8,128)S(1)} %get-tuple-element.78, f32[256,768]{1,0:T(8,128)S(1)} %collective-permute-done.25, bf16[768,1536]{1,0:T(8,128)(2,1)} %bitcast.17, bf16[512,1536]{1,0:T(8,128)(2,1)S(1)} %get-tuple-element.79, s32[]{:T(128)S(6)} %select_n.28, f32[768]{0:T(1024)S(1)} %get-tuple-element.57), kind=kOutput, calls=%fused_computation.30 | convolution fusion | flops 604766208 | bytes 5115908 | tf_op jit(solution)/shard_map/dot_general | solution.py:306
  160.3 3.9 %collective-permute-done.29 = bf16[2,1,2,2,48,384]{5,4,3,2,1,0:T(8,128)(2,1)S(1)} collective-permute-done((bf16[2,1,2,2,48,384]{5,4,3,2,1,0:T(8,128)(2,1)S(1)}, bf16[2,1,2,2,48,384]{5,4,3,2,1,0:T(8,128)(2,1)S(1)}, u32[]{:S(2)}, u32[]{:S(2)}) %collective-permute-start.29) | collective-permute-done | bytes 294944 | tf_op jit(solution)/shard_map/ppermute | solution.py:225
  165.1 8.3 %collective-permute-done.27 = bf16[2,2,1,2,48,1536]{5,4,3,2,1,0:T(8,128)(2,1)S(1)} collective-permute-done((bf16[2,2,1,2,48,1536]{5,4,3,2,1,0:T(8,128)(2,1)S(1)}, bf16[2,2,1,2,48,1536]{5,4,3,2,1,0:T(8,128)(2,1)S(1)}, u32[]{:S(2)}, u32[]{:S(2)}) %collective-permute-start.27) | collective-permute-done | bytes 1179680 | tf_op jit(solution)/shard_map/ppermute | solution.py:225
  173.4 1.8 convert_add_fusion.1
  175.2 6.8 %shard_map.204 = (bf16[512,1152]{1,0:T(8,128)(2,1)S(1)}, f32[1,8,384]{2,1,0:T(8,128)S(1)}) custom-call(bf16[512,1152]{1,0:T(8,128)(2,1)S(1)} %pad_maximum_fusion.1.stack_ref, s32[512,1]{1,0:T(8,128)S(1)} %copy.29.seg_column_ref, s32[1,1,512]{2,1,0:T(1,128)S(1)} %bitcast.87, f32[512,6]{1,0:T(8,128)S(1)} %get-tuple-element.41.log_ref, ...), custom_call_target="tpu_custom_call" | custom-call | flops 2013265920 | bytes 20000000 | tf_op jit(solution)/shard_map/pallas_call | solution.py:147
  182.1 1.8 convert_add_fusion
  198.0 1.8 collective-permute-start.49
  199.8 17.1 %collective-permute-done.49 = bf16[2,1,1,1,48,384]{5,4,3,2,1,0:T(8,128)(2,1)S(1)} collective-permute-done((bf16[2,1,1,1,48,384]{5,4,3,2,1,0:T(8,128)(2,1)S(1)}, bf16[2,1,1,1,48,384]{5,4,3,2,1,0:T(8,128)(2,1)S(1)}, u32[]{:S(2)}, u32[]{:S(2)}) %collective-permute-start.49) | collective-permute-done | bytes 73760 | tf_op jit(solution)/shard_map/ppermute | solution.py:225
  216.9 1.9 collective-permute-start.50
  218.8 3.1 %collective-permute-done.50 = bf16[1,1,1,1,48,384]{5,4,3,2,1,0:T(8,128)(2,1)S(1)} collective-permute-done((bf16[1,1,1,1,48,384]{5,4,3,2,1,0:T(8,128)(2,1)S(1)}, bf16[1,1,1,1,48,384]{5,4,3,2,1,0:T(8,128)(2,1)S(1)}, u32[]{:S(2)}, u32[]{:S(2)}) %collective-permute-start.50) | collective-permute-done | bytes 36896 | tf_op jit(solution)/shard_map/ppermute | solution.py:225
  225.5 3.2 %collective-permute-done.36 = bf16[2,1,2,2,48,384]{5,4,3,2,1,0:T(8,128)(2,1)S(1)} collective-permute-done((bf16[2,1,2,2,48,384]{5,4,3,2,1,0:T(8,128)(2,1)S(1)}, bf16[2,1,2,2,48,384]{5,4,3,2,1,0:T(8,128)(2,1)S(1)}, u32[]{:S(2)}, u32[]{:S(2)}) %collective-permute-start.36) | collective-permute-done | bytes 294944 | tf_op jit(solution)/shard_map/ppermute | solution.py:225
  230.1 3.1 %collective-permute-done.40 = bf16[2,2,2,1,48,384]{5,4,3,2,1,0:T(8,128)(2,1)S(1)} collective-permute-done((bf16[2,2,2,1,48,384]{5,4,3,2,1,0:T(8,128)(2,1)S(1)}, bf16[2,2,2,1,48,384]{5,4,3,2,1,0:T(8,128)(2,1)S(1)}, u32[]{:S(2)}, u32[]{:S(2)}) %collective-permute-start.40) | collective-permute-done | bytes 294944 | tf_op jit(solution)/shard_map/ppermute | solution.py:225
  236.5 1.9 collective-permute-done.37
  244.3 2.0 collective-permute-start.47
  247.1 1.8 collective-permute-start.39
  249.2 2.1 collective-permute-start.43
  252.1 2.1 collective-permute-done.43
  255.1 1.9 collective-permute-start.55
  261.4 2.5 collective-permute-done.32
  267.8 1.8 collective-permute-start.34
  269.7 2.3 collective-permute-start.56
  272.1 2.1 collective-permute-start.35
  275.2 7.6 %collective-permute-done.35 = f32[6912]{0:T(1024)S(1)} collective-permute-done((f32[6912]{0:T(1024)S(1)}, f32[6912]{0:T(1024)S(1)}, u32[]{:S(2)}, u32[]{:S(2)}) %collective-permute-start.35) | collective-permute-done | bytes 27680 | tf_op jit(solution)/shard_map/ppermute | solution.py:245
  (318 shorter events, 106.2 us)
Async XLA Ops:
  0.7 25.1 %collective-permute-start.9 = (bf16[1,1,1,1,48,384]{5,4,3,2,1,0:T(8,128)(2,1)}, bf16[1,1,1,1,48,384]{5,4,3,2,1,0:T(8,128)(2,1)}, u32[]{:S(2)}, u32[]{:S(2)}) collective-permute-start(bf16[1,1,1,1,48,384]{5,4,3,2,1,0:T(8,128)(2,1)} %bitcast.114), channel_id=1, source_target_pairs={{0,16},{2,18},{4,20},{6,22},{8,24},{10,26},{12,28},{14,30},{16,0},... | collective-permute-start | bytes 110600 | tf_op jit(solution)/shard_map/ppermute | solution.py:196
  6.2 22.0 %collective-permute-start.6 = (bf16[1,1,1,1,48,384]{5,4,3,2,1,0:T(8,128)(2,1)S(1)}, bf16[1,1,1,1,48,384]{5,4,3,2,1,0:T(8,128)(2,1)}, u32[]{:S(2)}, u32[]{:S(2)}) collective-permute-start(bf16[1,1,1,1,48,384]{5,4,3,2,1,0:T(8,128)(2,1)S(1)} %get-tuple-element.70), channel_id=1, source_target_pairs={{0,16},{2,18},{4,20},{6,22},{8,24},{10,26},{12,28},{14,30},{16,0},... | collective-permute-start | bytes 110600 | tf_op jit(solution)/shard_map/ppermute | solution.py:196
  6.2 16.8 %collective-permute-start = (bf16[1,1,1,1,48,384]{5,4,3,2,1,0:T(8,128)(2,1)S(1)}, bf16[1,1,1,1,48,384]{5,4,3,2,1,0:T(8,128)(2,1)}, u32[]{:S(2)}, u32[]{:S(2)}) collective-permute-start(bf16[1,1,1,1,48,384]{5,4,3,2,1,0:T(8,128)(2,1)S(1)} %get-tuple-element.71), channel_id=1, source_target_pairs={{0,16},{2,18},{4,20},{6,22},{8,24},{10,26},{12,28},{14,30},{16,0},... | collective-permute-start | bytes 110600 | tf_op jit(solution)/shard_map/ppermute | solution.py:196
  9.1 13.0 %collective-permute-start.3 = (bf16[1,1,1,1,48,384]{5,4,3,2,1,0:T(8,128)(2,1)}, bf16[1,1,1,1,48,384]{5,4,3,2,1,0:T(8,128)(2,1)}, u32[]{:S(2)}, u32[]{:S(2)}) collective-permute-start(bf16[1,1,1,1,48,384]{5,4,3,2,1,0:T(8,128)(2,1)} %get-tuple-element.72), channel_id=1, source_target_pairs={{0,16},{2,18},{4,20},{6,22},{8,24},{10,26},{12,28},{14,30},{16,0},... | collective-permute-start | bytes 110600 | tf_op jit(solution)/shard_map/ppermute | solution.py:196
  9.2 28.9 %collective-permute-start.13 = (bf16[1,1,1,1,48,1536]{5,4,3,2,1,0:T(8,128)(2,1)}, bf16[1,1,1,1,48,1536]{5,4,3,2,1,0:T(8,128)(2,1)}, u32[]{:S(2)}, u32[]{:S(2)}) collective-permute-start(bf16[1,1,1,1,48,1536]{5,4,3,2,1,0:T(8,128)(2,1)} %bitcast.113), channel_id=1, source_target_pairs={{0,16},{2,18},{4,20},{6,22},{8,24},{10,26},{12,28},{14,30},{16,0},... | collective-permute-start | bytes 442376 | tf_op jit(solution)/shard_map/ppermute | solution.py:196
  22.1 14.0 %collective-permute-start.11 = (bf16[1,1,1,1,48,1536]{5,4,3,2,1,0:T(8,128)(2,1)S(1)}, bf16[1,1,1,1,48,1536]{5,4,3,2,1,0:T(8,128)(2,1)S(1)}, u32[]{:S(2)}, u32[]{:S(2)}) collective-permute-start(bf16[1,1,1,1,48,1536]{5,4,3,2,1,0:T(8,128)(2,1)S(1)} %bitcast.112), channel_id=1, source_target_pairs={{0,16},{2,18},{4,20},{6,22},{8,24},{10,26},{12,28},{14,30},{16,0},... | collective-permute-start | bytes 442376 | tf_op jit(solution)/shard_map/ppermute | solution.py:196
  23.0 6.5 %collective-permute-start.4 = (bf16[2,1,1,1,48,384]{5,4,3,2,1,0:T(8,128)(2,1)S(1)}, bf16[2,1,1,1,48,384]{5,4,3,2,1,0:T(8,128)(2,1)S(1)}, u32[]{:S(2)}, u32[]{:S(2)}) collective-permute-start(bf16[2,1,1,1,48,384]{5,4,3,2,1,0:T(8,128)(2,1)S(1)} %constant_dynamic-slice_fusion.14), channel_id=1, source_target_pairs={{0,8},{2,10},{4,12},{6,14},{8,0},{10,2},{12,4},{14,6},{16,24},{18,... | collective-permute-start | bytes 221192 | tf_op jit(solution)/shard_map/ppermute | solution.py:196
  25.8 4.9 %collective-permute-start.1 = (bf16[2,1,1,1,48,384]{5,4,3,2,1,0:T(8,128)(2,1)S(1)}, bf16[2,1,1,1,48,384]{5,4,3,2,1,0:T(8,128)(2,1)S(1)}, u32[]{:S(2)}, u32[]{:S(2)}) collective-permute-start(bf16[2,1,1,1,48,384]{5,4,3,2,1,0:T(8,128)(2,1)S(1)} %constant_dynamic-slice_fusion.17), channel_id=1, source_target_pairs={{0,4},{2,6},{4,0},{6,2},{8,12},{10,14},{12,8},{14,10},{16,20},{18,... | collective-permute-start | bytes 221192 | tf_op jit(solution)/shard_map/ppermute | solution.py:196
  28.2 7.3 %collective-permute-start.10 = (bf16[2,1,1,1,48,384]{5,4,3,2,1,0:T(8,128)(2,1)S(1)}, bf16[2,1,1,1,48,384]{5,4,3,2,1,0:T(8,128)(2,1)S(1)}, u32[]{:S(2)}, u32[]{:S(2)}) collective-permute-start(bf16[2,1,1,1,48,384]{5,4,3,2,1,0:T(8,128)(2,1)S(1)} %constant_dynamic-slice_fusion.8), channel_id=1, source_target_pairs={{0,4},{2,6},{4,0},{6,2},{8,12},{10,14},{12,8},{14,10},{16,20},{18,... | collective-permute-start | bytes 221192 | tf_op jit(solution)/shard_map/ppermute | solution.py:196
  30.7 11.9 %collective-permute-start.5 = (bf16[2,2,1,1,48,384]{5,4,3,2,1,0:T(8,128)(2,1)S(1)}, bf16[2,2,1,1,48,384]{5,4,3,2,1,0:T(8,128)(2,1)S(1)}, u32[]{:S(2)}, u32[]{:S(2)}) collective-permute-start(bf16[2,2,1,1,48,384]{5,4,3,2,1,0:T(8,128)(2,1)S(1)} %constant_dynamic-slice_fusion.13), channel_id=1, source_target_pairs={{0,4},{2,6},{4,0},{6,2},{8,12},{10,14},{12,8},{14,10},{16,20},{18,... | collective-permute-start | bytes 442376 | tf_op jit(solution)/shard_map/ppermute | solution.py:196
  34.0 8.6 %collective-permute-start.2 = (bf16[2,1,2,1,48,384]{5,4,3,2,1,0:T(8,128)(2,1)S(1)}, bf16[2,1,2,1,48,384]{5,4,3,2,1,0:T(8,128)(2,1)S(1)}, u32[]{:S(2)}, u32[]{:S(2)}) collective-permute-start(bf16[2,1,2,1,48,384]{5,4,3,2,1,0:T(8,128)(2,1)S(1)} %constant_dynamic-slice_fusion.16), channel_id=1, source_target_pairs={{0,2},{2,0},{4,6},{6,4},{8,10},{10,8},{12,14},{14,12},{16,18},{18,... | collective-permute-start | bytes 442376 | tf_op jit(solution)/shard_map/ppermute | solution.py:196
  35.5 7.2 %collective-permute-start.8 = (bf16[2,2,1,1,48,384]{5,4,3,2,1,0:T(8,128)(2,1)S(1)}, bf16[2,2,1,1,48,384]{5,4,3,2,1,0:T(8,128)(2,1)S(1)}, u32[]{:S(2)}, u32[]{:S(2)}) collective-permute-start(bf16[2,2,1,1,48,384]{5,4,3,2,1,0:T(8,128)(2,1)S(1)} %constant_dynamic-slice_fusion.10), channel_id=1, source_target_pairs={{0,2},{2,0},{4,6},{6,4},{8,10},{10,8},{12,14},{14,12},{16,18},{18,... | collective-permute-start | bytes 442376 | tf_op jit(solution)/shard_map/ppermute | solution.py:196
  37.8 8.7 %collective-permute-start.12 = (bf16[2,1,1,1,48,1536]{5,4,3,2,1,0:T(8,128)(2,1)S(1)}, bf16[2,1,1,1,48,1536]{5,4,3,2,1,0:T(8,128)(2,1)S(1)}, u32[]{:S(2)}, u32[]{:S(2)}) collective-permute-start(bf16[2,1,1,1,48,1536]{5,4,3,2,1,0:T(8,128)(2,1)S(1)} %constant_dynamic-slice_fusion.6), channel_id=1, source_target_pairs={{0,8},{2,10},{4,12},{6,14},{8,0},{10,2},{12,4},{14,6},{16,24},{18,... | collective-permute-start | bytes 884744 | tf_op jit(solution)/shard_map/ppermute | solution.py:196
  40.6 9.0 %collective-permute-start.14 = (bf16[2,1,1,1,48,1536]{5,4,3,2,1,0:T(8,128)(2,1)S(1)}, bf16[2,1,1,1,48,1536]{5,4,3,2,1,0:T(8,128)(2,1)S(1)}, u32[]{:S(2)}, u32[]{:S(2)}) collective-permute-start(bf16[2,1,1,1,48,1536]{5,4,3,2,1,0:T(8,128)(2,1)S(1)} %constant_dynamic-slice_fusion.4), channel_id=1, source_target_pairs={{0,8},{2,10},{4,12},{6,14},{8,0},{10,2},{12,4},{14,6},{16,24},{18,... | collective-permute-start | bytes 884744 | tf_op jit(solution)/shard_map/ppermute | solution.py:196
  51.5 7.8 %collective-permute-start.18 = (bf16[2,1,2,1,48,384]{5,4,3,2,1,0:T(8,128)(2,1)S(1)}, bf16[2,1,2,1,48,384]{5,4,3,2,1,0:T(8,128)(2,1)S(1)}, u32[]{:S(2)}, u32[]{:S(2)}) collective-permute-start(bf16[2,1,2,1,48,384]{5,4,3,2,1,0:T(8,128)(2,1)S(1)} %constant_dynamic-slice_fusion.7), channel_id=1, source_target_pairs={{0,2},{2,0},{4,6},{6,4},{8,10},{10,8},{12,14},{14,12},{16,18},{18,... | collective-permute-start | bytes 442376 | tf_op jit(solution)/shard_map/ppermute | solution.py:196
  55.4 9.9 %collective-permute-start.16 = (bf16[2,2,2,1,48,384]{5,4,3,2,1,0:T(8,128)(2,1)S(1)}, bf16[2,2,2,1,48,384]{5,4,3,2,1,0:T(8,128)(2,1)S(1)}, u32[]{:S(2)}, u32[]{:S(2)}) collective-permute-start(bf16[2,2,2,1,48,384]{5,4,3,2,1,0:T(8,128)(2,1)S(1)} %constant_dynamic-slice_fusion.12), channel_id=1, source_target_pairs={{0,2},{2,0},{4,6},{6,4},{8,10},{10,8},{12,14},{14,12},{16,18},{18,... | collective-permute-start | bytes 884744 | tf_op jit(solution)/shard_map/ppermute | solution.py:196
  56.0 11.8 %collective-permute-start.15 = (bf16[2,1,2,2,48,384]{5,4,3,2,1,0:T(8,128)(2,1)S(1)}, bf16[2,1,2,2,48,384]{5,4,3,2,1,0:T(8,128)(2,1)S(1)}, u32[]{:S(2)}, u32[]{:S(2)}) collective-permute-start(bf16[2,1,2,2,48,384]{5,4,3,2,1,0:T(8,128)(2,1)S(1)} %constant_dynamic-slice_fusion.15), channel_id=1, source_target_pairs={{0,8},{2,10},{4,12},{6,14},{8,0},{10,2},{12,4},{14,6},{16,24},{18,... | collective-permute-start | bytes 884744 | tf_op jit(solution)/shard_map/ppermute | solution.py:196
  57.3 9.9 %collective-permute-start.17 = (bf16[2,2,1,2,48,384]{5,4,3,2,1,0:T(8,128)(2,1)S(1)}, bf16[2,2,1,2,48,384]{5,4,3,2,1,0:T(8,128)(2,1)S(1)}, u32[]{:S(2)}, u32[]{:S(2)}) collective-permute-start(bf16[2,2,1,2,48,384]{5,4,3,2,1,0:T(8,128)(2,1)S(1)} %constant_dynamic-slice_fusion.9), channel_id=1, source_target_pairs={{0,4},{2,6},{4,0},{6,2},{8,12},{10,14},{12,8},{14,10},{16,20},{18,... | collective-permute-start | bytes 884744 | tf_op jit(solution)/shard_map/ppermute | solution.py:196
  59.1 21.3 %collective-permute-start.19 = (bf16[2,2,1,1,48,1536]{5,4,3,2,1,0:T(8,128)(2,1)S(1)}, bf16[2,2,1,1,48,1536]{5,4,3,2,1,0:T(8,128)(2,1)S(1)}, u32[]{:S(2)}, u32[]{:S(2)}) collective-permute-start(bf16[2,2,1,1,48,1536]{5,4,3,2,1,0:T(8,128)(2,1)S(1)} %constant_dynamic-slice_fusion.5), channel_id=1, source_target_pairs={{0,4},{2,6},{4,0},{6,2},{8,12},{10,14},{12,8},{14,10},{16,20},{18,... | collective-permute-start | bytes 1769480 | tf_op jit(solution)/shard_map/ppermute | solution.py:196
  59.3 17.8 %collective-permute-start.20 = (bf16[2,2,1,1,48,1536]{5,4,3,2,1,0:T(8,128)(2,1)S(1)}, bf16[2,2,1,1,48,1536]{5,4,3,2,1,0:T(8,128)(2,1)S(1)}, u32[]{:S(2)}, u32[]{:S(2)}) collective-permute-start(bf16[2,2,1,1,48,1536]{5,4,3,2,1,0:T(8,128)(2,1)S(1)} %constant_dynamic-slice_fusion.3), channel_id=1, source_target_pairs={{0,2},{2,0},{4,6},{6,4},{8,10},{10,8},{12,14},{14,12},{16,18},{18,... | collective-permute-start | bytes 1769480 | tf_op jit(solution)/shard_map/ppermute | solution.py:196
  83.6 8.5 %collective-permute-start.21 = (bf16[2,1,2,2,48,384]{5,4,3,2,1,0:T(8,128)(2,1)}, bf16[2,1,2,2,48,384]{5,4,3,2,1,0:T(8,128)(2,1)}, u32[]{:S(2)}, u32[]{:S(2)}) collective-permute-start(bf16[2,1,2,2,48,384]{5,4,3,2,1,0:T(8,128)(2,1)} %constant_dynamic-slice_fusion.2), channel_id=1, source_target_pairs={{0,8},{2,10},{4,12},{6,14},{8,0},{10,2},{12,4},{14,6},{16,24},{18,... | collective-permute-start | bytes 884744 | tf_op jit(solution)/shard_map/ppermute | solution.py:196
  94.5 5.4 %collective-permute-start.22 = (f32[256,768]{1,0:T(8,128)}, f32[256,768]{1,0:T(8,128)}, u32[]{:S(2)}, u32[]{:S(2)}) collective-permute-start(f32[256,768]{1,0:T(8,128)} %fusion.42), channel_id=1, source_target_pairs={{0,1},{1,0},{2,3},{3,2},{4,5},{5,4},{6,7},{7,6},{8,9},{9,8},{10,11... | collective-permute-start | bytes 2359304 | tf_op jit(solution)/shard_map/ppermute | solution.py:310
  97.5 28.3 %collective-permute-start.23 = (bf16[2,2,2,1,48,1536]{5,4,3,2,1,0:T(8,128)(2,1)}, bf16[2,2,2,1,48,1536]{5,4,3,2,1,0:T(8,128)(2,1)S(1)}, u32[]{:S(2)}, u32[]{:S(2)}) collective-permute-start(bf16[2,2,2,1,48,1536]{5,4,3,2,1,0:T(8,128)(2,1)} %constant_dynamic-slice_fusion.1), channel_id=1, source_target_pairs={{0,2},{2,0},{4,6},{6,4},{8,10},{10,8},{12,14},{14,12},{16,18},{18,... | collective-permute-start | bytes 3538952 | tf_op jit(solution)/shard_map/ppermute | solution.py:196
  98.1 32.5 %collective-permute-start.24 = (bf16[2,2,1,2,48,1536]{5,4,3,2,1,0:T(8,128)(2,1)}, bf16[2,2,1,2,48,1536]{5,4,3,2,1,0:T(8,128)(2,1)S(1)}, u32[]{:S(2)}, u32[]{:S(2)}) collective-permute-start(bf16[2,2,1,2,48,1536]{5,4,3,2,1,0:T(8,128)(2,1)} %constant_dynamic-slice_fusion), channel_id=1, source_target_pairs={{0,4},{2,6},{4,0},{6,2},{8,12},{10,14},{12,8},{14,10},{16,20},{18,... | collective-permute-start | bytes 3538952 | tf_op jit(solution)/shard_map/ppermute | solution.py:196
  142.7 13.7 %collective-permute-start.25 = (f32[256,768]{1,0:T(8,128)S(1)}, f32[256,768]{1,0:T(8,128)S(1)}, u32[]{:S(2)}, u32[]{:S(2)}) collective-permute-start(f32[256,768]{1,0:T(8,128)S(1)} %fusion.30), channel_id=1, source_target_pairs={{0,1},{1,0},{2,3},{3,2},{4,5},{5,4},{6,7},{7,6},{8,9},{9,8},{10,11... | collective-permute-start | bytes 2359304 | tf_op jit(solution)/shard_map/ppermute | solution.py:310
  143.4 38.7 %collective-permute-start.28 = (bf16[2,2,2,1,48,1536]{5,4,3,2,1,0:T(8,128)(2,1)S(1)}, bf16[2,2,2,1,48,1536]{5,4,3,2,1,0:T(8,128)(2,1)S(1)}, u32[]{:S(2)}, u32[]{:S(2)}) collective-permute-start(bf16[2,2,2,1,48,1536]{5,4,3,2,1,0:T(8,128)(2,1)S(1)} %dynamic-slice_convert_fusion), channel_id=1, source_target_pairs={{0,2},{2,0},{4,6},{6,4},{8,10},{10,8},{12,14},{14,12},{16,18},{18,... | collective-permute-start | bytes 3538952 | tf_op jit(solution)/shard_map/ppermute | solution.py:225
  145.6 27.8 %collective-permute-start.27 = (bf16[2,2,1,2,48,1536]{5,4,3,2,1,0:T(8,128)(2,1)S(1)}, bf16[2,2,1,2,48,1536]{5,4,3,2,1,0:T(8,128)(2,1)S(1)}, u32[]{:S(2)}, u32[]{:S(2)}) collective-permute-start(bf16[2,2,1,2,48,1536]{5,4,3,2,1,0:T(8,128)(2,1)S(1)} %dynamic-slice_convert_fusion.1), channel_id=1, source_target_pairs={{0,4},{2,6},{4,0},{6,2},{8,12},{10,14},{12,8},{14,10},{16,20},{18,... | collective-permute-start | bytes 3538952 | tf_op jit(solution)/shard_map/ppermute | solution.py:225
  155.1 9.1 %collective-permute-start.29 = (bf16[2,1,2,2,48,384]{5,4,3,2,1,0:T(8,128)(2,1)S(1)}, bf16[2,1,2,2,48,384]{5,4,3,2,1,0:T(8,128)(2,1)S(1)}, u32[]{:S(2)}, u32[]{:S(2)}) collective-permute-start(bf16[2,1,2,2,48,384]{5,4,3,2,1,0:T(8,128)(2,1)S(1)} %dynamic-slice_convert_fusion.9), channel_id=1, source_target_pairs={{0,8},{2,10},{4,12},{6,14},{8,0},{10,2},{12,4},{14,6},{16,24},{18,... | collective-permute-start | bytes 884744 | tf_op jit(solution)/shard_map/ppermute | solution.py:225
  190.2 7.7 %collective-permute-start.48 = (bf16[2,1,2,1,48,384]{5,4,3,2,1,0:T(8,128)(2,1)S(1)}, bf16[2,1,2,1,48,384]{5,4,3,2,1,0:T(8,128)(2,1)S(1)}, u32[]{:S(2)}, u32[]{:S(2)}) collective-permute-start(bf16[2,1,2,1,48,384]{5,4,3,2,1,0:T(8,128)(2,1)S(1)} %dynamic-slice_convert_fusion.12), channel_id=1, source_target_pairs={{0,2},{2,0},{4,6},{6,4},{8,10},{10,8},{12,14},{14,12},{16,18},{18,... | collective-permute-start | bytes 442376 | tf_op jit(solution)/shard_map/ppermute | solution.py:225
  194.5 60.4 %collective-permute-start.54 = (bf16[2,2,1,1,48,1536]{5,4,3,2,1,0:T(8,128)(2,1)S(1)}, bf16[2,2,1,1,48,1536]{5,4,3,2,1,0:T(8,128)(2,1)S(1)}, u32[]{:S(2)}, u32[]{:S(2)}) collective-permute-start(bf16[2,2,1,1,48,1536]{5,4,3,2,1,0:T(8,128)(2,1)S(1)} %dynamic-slice_convert_fusion.2), channel_id=1, source_target_pairs={{0,2},{2,0},{4,6},{6,4},{8,10},{10,8},{12,14},{14,12},{16,18},{18,... | collective-permute-start | bytes 1769480 | tf_op jit(solution)/shard_map/ppermute | solution.py:225
  195.1 61.9 %collective-permute-start.51 = (bf16[2,2,1,1,48,1536]{5,4,3,2,1,0:T(8,128)(2,1)S(1)}, bf16[2,2,1,1,48,1536]{5,4,3,2,1,0:T(8,128)(2,1)S(1)}, u32[]{:S(2)}, u32[]{:S(2)}) collective-permute-start(bf16[2,2,1,1,48,1536]{5,4,3,2,1,0:T(8,128)(2,1)S(1)} %dynamic-slice_convert_fusion.3), channel_id=1, source_target_pairs={{0,4},{2,6},{4,0},{6,2},{8,12},{10,14},{12,8},{14,10},{16,20},{18,... | collective-permute-start | bytes 1769480 | tf_op jit(solution)/shard_map/ppermute | solution.py:225
  196.9 60.7 %collective-permute-start.30 = (f32[256,768]{1,0:T(8,128)S(1)}, f32[256,768]{1,0:T(8,128)S(1)}, u32[]{:S(2)}, u32[]{:S(2)}) collective-permute-start(f32[256,768]{1,0:T(8,128)S(1)} %copy-done.38), channel_id=1, source_target_pairs={{0,1},{1,0},{2,3},{3,2},{4,5},{5,4},{6,7},{7,6},{8,9},{9,8},{10,11... | collective-permute-start | bytes 2359304 | tf_op jit(solution)/shard_map/ppermute | solution.py:310
  196.9 27.1 %collective-permute-start.44 = (bf16[2,2,1,2,48,384]{5,4,3,2,1,0:T(8,128)(2,1)S(1)}, bf16[2,2,1,2,48,384]{5,4,3,2,1,0:T(8,128)(2,1)S(1)}, u32[]{:S(2)}, u32[]{:S(2)}) collective-permute-start(bf16[2,2,1,2,48,384]{5,4,3,2,1,0:T(8,128)(2,1)S(1)} %dynamic-slice_convert_fusion.6), channel_id=1, source_target_pairs={{0,4},{2,6},{4,0},{6,2},{8,12},{10,14},{12,8},{14,10},{16,20},{18,... | collective-permute-start | bytes 884744 | tf_op jit(solution)/shard_map/ppermute | solution.py:225
  198.0 18.9 %collective-permute-start.49 = (bf16[2,1,1,1,48,384]{5,4,3,2,1,0:T(8,128)(2,1)S(1)}, bf16[2,1,1,1,48,384]{5,4,3,2,1,0:T(8,128)(2,1)S(1)}, u32[]{:S(2)}, u32[]{:S(2)}) collective-permute-start(bf16[2,1,1,1,48,384]{5,4,3,2,1,0:T(8,128)(2,1)S(1)} %dynamic-slice_convert_fusion.16), channel_id=1, source_target_pairs={{0,4},{2,6},{4,0},{6,2},{8,12},{10,14},{12,8},{14,10},{16,20},{18,... | collective-permute-start | bytes 221192 | tf_op jit(solution)/shard_map/ppermute | solution.py:225
  216.9 5.0 %collective-permute-start.50 = (bf16[1,1,1,1,48,384]{5,4,3,2,1,0:T(8,128)(2,1)S(1)}, bf16[1,1,1,1,48,384]{5,4,3,2,1,0:T(8,128)(2,1)S(1)}, u32[]{:S(2)}, u32[]{:S(2)}) collective-permute-start(bf16[1,1,1,1,48,384]{5,4,3,2,1,0:T(8,128)(2,1)S(1)} %dynamic-slice_convert_fusion.20), channel_id=1, source_target_pairs={{0,16},{2,18},{4,20},{6,22},{8,24},{10,26},{12,28},{14,30},{16,0},... | collective-permute-start | bytes 110600 | tf_op jit(solution)/shard_map/ppermute | solution.py:225
  221.9 6.7 %collective-permute-start.36 = (bf16[2,1,2,2,48,384]{5,4,3,2,1,0:T(8,128)(2,1)S(1)}, bf16[2,1,2,2,48,384]{5,4,3,2,1,0:T(8,128)(2,1)S(1)}, u32[]{:S(2)}, u32[]{:S(2)}) collective-permute-start(bf16[2,1,2,2,48,384]{5,4,3,2,1,0:T(8,128)(2,1)S(1)} %dynamic-slice_convert_fusion.8), channel_id=1, source_target_pairs={{0,8},{2,10},{4,12},{6,14},{8,0},{10,2},{12,4},{14,6},{16,24},{18,... | collective-permute-start | bytes 884744 | tf_op jit(solution)/shard_map/ppermute | solution.py:225
  224.1 9.2 %collective-permute-start.40 = (bf16[2,2,2,1,48,384]{5,4,3,2,1,0:T(8,128)(2,1)S(1)}, bf16[2,2,2,1,48,384]{5,4,3,2,1,0:T(8,128)(2,1)S(1)}, u32[]{:S(2)}, u32[]{:S(2)}) collective-permute-start(bf16[2,2,2,1,48,384]{5,4,3,2,1,0:T(8,128)(2,1)S(1)} %dynamic-slice_convert_fusion.7), channel_id=1, source_target_pairs={{0,2},{2,0},{4,6},{6,4},{8,10},{10,8},{12,14},{14,12},{16,18},{18,... | collective-permute-start | bytes 884744 | tf_op jit(solution)/shard_map/ppermute | solution.py:225
  228.6 6.2 %collective-permute-start.45 = (bf16[2,2,1,1,48,384]{5,4,3,2,1,0:T(8,128)(2,1)S(1)}, bf16[2,2,1,1,48,384]{5,4,3,2,1,0:T(8,128)(2,1)S(1)}, u32[]{:S(2)}, u32[]{:S(2)}) collective-permute-start(bf16[2,2,1,1,48,384]{5,4,3,2,1,0:T(8,128)(2,1)S(1)} %dynamic-slice_convert_fusion.13), channel_id=1, source_target_pairs={{0,2},{2,0},{4,6},{6,4},{8,10},{10,8},{12,14},{14,12},{16,18},{18,... | collective-permute-start | bytes 442376 | tf_op jit(solution)/shard_map/ppermute | solution.py:225
  233.2 5.1 %collective-permute-start.37 = (bf16[2,1,2,1,48,384]{5,4,3,2,1,0:T(8,128)(2,1)S(1)}, bf16[2,1,2,1,48,384]{5,4,3,2,1,0:T(8,128)(2,1)S(1)}, u32[]{:S(2)}, u32[]{:S(2)}) collective-permute-start(bf16[2,1,2,1,48,384]{5,4,3,2,1,0:T(8,128)(2,1)S(1)} %dynamic-slice_convert_fusion.15), channel_id=1, source_target_pairs={{0,2},{2,0},{4,6},{6,4},{8,10},{10,8},{12,14},{14,12},{16,18},{18,... | collective-permute-start | bytes 442376 | tf_op jit(solution)/shard_map/ppermute | solution.py:225
  234.8 5.1 %collective-permute-start.41 = (bf16[2,2,1,1,48,384]{5,4,3,2,1,0:T(8,128)(2,1)S(1)}, bf16[2,2,1,1,48,384]{5,4,3,2,1,0:T(8,128)(2,1)S(1)}, u32[]{:S(2)}, u32[]{:S(2)}) collective-permute-start(bf16[2,2,1,1,48,384]{5,4,3,2,1,0:T(8,128)(2,1)S(1)} %dynamic-slice_convert_fusion.14), channel_id=1, source_target_pairs={{0,4},{2,6},{4,0},{6,2},{8,12},{10,14},{12,8},{14,10},{16,20},{18,... | collective-permute-start | bytes 442376 | tf_op jit(solution)/shard_map/ppermute | solution.py:225
  244.3 4.9 %collective-permute-start.47 = (bf16[1,1,1,1,48,384]{5,4,3,2,1,0:T(8,128)(2,1)S(1)}, bf16[1,1,1,1,48,384]{5,4,3,2,1,0:T(8,128)(2,1)S(1)}, u32[]{:S(2)}, u32[]{:S(2)}) collective-permute-start(bf16[1,1,1,1,48,384]{5,4,3,2,1,0:T(8,128)(2,1)S(1)} %dynamic-slice_convert_fusion.21), channel_id=1, source_target_pairs={{0,16},{2,18},{4,20},{6,22},{8,24},{10,26},{12,28},{14,30},{16,0},... | collective-permute-start | bytes 110600 | tf_op jit(solution)/shard_map/ppermute | solution.py:225
  247.1 5.0 %collective-permute-start.39 = (bf16[1,1,1,1,48,384]{5,4,3,2,1,0:T(8,128)(2,1)S(1)}, bf16[1,1,1,1,48,384]{5,4,3,2,1,0:T(8,128)(2,1)S(1)}, u32[]{:S(2)}, u32[]{:S(2)}) collective-permute-start(bf16[1,1,1,1,48,384]{5,4,3,2,1,0:T(8,128)(2,1)S(1)} %dynamic-slice_convert_fusion.23), channel_id=1, source_target_pairs={{0,16},{2,18},{4,20},{6,22},{8,24},{10,26},{12,28},{14,30},{16,0},... | collective-permute-start | bytes 110600 | tf_op jit(solution)/shard_map/ppermute | solution.py:225
  249.2 5.0 %collective-permute-start.43 = (bf16[1,1,1,1,48,384]{5,4,3,2,1,0:T(8,128)(2,1)S(1)}, bf16[1,1,1,1,48,384]{5,4,3,2,1,0:T(8,128)(2,1)S(1)}, u32[]{:S(2)}, u32[]{:S(2)}) collective-permute-start(bf16[1,1,1,1,48,384]{5,4,3,2,1,0:T(8,128)(2,1)S(1)} %dynamic-slice_convert_fusion.22), channel_id=1, source_target_pairs={{0,16},{2,18},{4,20},{6,22},{8,24},{10,26},{12,28},{14,30},{16,0},... | collective-permute-start | bytes 110600 | tf_op jit(solution)/shard_map/ppermute | solution.py:225
  255.1 14.5 %collective-permute-start.55 = (bf16[2,1,1,1,48,1536]{5,4,3,2,1,0:T(8,128)(2,1)S(1)}, bf16[2,1,1,1,48,1536]{5,4,3,2,1,0:T(8,128)(2,1)S(1)}, u32[]{:S(2)}, u32[]{:S(2)}) collective-permute-start(bf16[2,1,1,1,48,1536]{5,4,3,2,1,0:T(8,128)(2,1)S(1)} %dynamic-slice_convert_fusion.4), channel_id=1, source_target_pairs={{0,8},{2,10},{4,12},{6,14},{8,0},{10,2},{12,4},{14,6},{16,24},{18,... | collective-permute-start | bytes 884744 | tf_op jit(solution)/shard_map/ppermute | solution.py:225
  257.2 14.8 %collective-permute-start.52 = (bf16[2,1,1,1,48,1536]{5,4,3,2,1,0:T(8,128)(2,1)S(1)}, bf16[2,1,1,1,48,1536]{5,4,3,2,1,0:T(8,128)(2,1)S(1)}, u32[]{:S(2)}, u32[]{:S(2)}) collective-permute-start(bf16[2,1,1,1,48,1536]{5,4,3,2,1,0:T(8,128)(2,1)S(1)} %dynamic-slice_convert_fusion.5), channel_id=1, source_target_pairs={{0,8},{2,10},{4,12},{6,14},{8,0},{10,2},{12,4},{14,6},{16,24},{18,... | collective-permute-start | bytes 884744 | tf_op jit(solution)/shard_map/ppermute | solution.py:225
  269.7 16.1 %collective-permute-start.56 = (bf16[1,1,1,1,48,1536]{5,4,3,2,1,0:T(8,128)(2,1)S(1)}, bf16[1,1,1,1,48,1536]{5,4,3,2,1,0:T(8,128)(2,1)S(1)}, u32[]{:S(2)}, u32[]{:S(2)}) collective-permute-start(bf16[1,1,1,1,48,1536]{5,4,3,2,1,0:T(8,128)(2,1)S(1)} %dynamic-slice_convert_fusion.10), channel_id=1, source_target_pairs={{0,16},{2,18},{4,20},{6,22},{8,24},{10,26},{12,28},{14,30},{16,0},... | collective-permute-start | bytes 442376 | tf_op jit(solution)/shard_map/ppermute | solution.py:225
  272.1 10.7 %collective-permute-start.35 = (f32[6912]{0:T(1024)S(1)}, f32[6912]{0:T(1024)S(1)}, u32[]{:S(2)}, u32[]{:S(2)}) collective-permute-start(f32[6912]{0:T(1024)S(1)} %add.204), channel_id=1, source_target_pairs={{0,16},{2,18},{4,20},{6,22},{8,24},{10,26},{12,28},{14,30},{16,0},... | collective-permute-start | bytes 82952 | tf_op jit(solution)/shard_map/ppermute | solution.py:245
  274.2 12.4 %collective-permute-start.53 = (bf16[1,1,1,1,48,1536]{5,4,3,2,1,0:T(8,128)(2,1)S(1)}, bf16[1,1,1,1,48,1536]{5,4,3,2,1,0:T(8,128)(2,1)S(1)}, u32[]{:S(2)}, u32[]{:S(2)}) collective-permute-start(bf16[1,1,1,1,48,1536]{5,4,3,2,1,0:T(8,128)(2,1)S(1)} %dynamic-slice_convert_fusion.11), channel_id=1, source_target_pairs={{0,16},{2,18},{4,20},{6,22},{8,24},{10,26},{12,28},{14,30},{16,0},... | collective-permute-start | bytes 442376 | tf_op jit(solution)/shard_map/ppermute | solution.py:225
  (49 other events, 269.8 us)
where the time goes:
time: 289 us; the launch traced here: 287 us
  waiting for transfers between devices  103 us (36%)
  starting transfers between devices  72.1 us (25%)
  local copies, waits for them, and re-layouts  39.1 us (14%)
  matrix products  35.1 us (12%)
  other arithmetic  13.5 us (5%)
  Pallas kernels  12.4 us (4%)
  blocking collectives  10.3 us (4%)
    ppermute x24, waiting for transfers between devices, step(): lax.ppermute(away.astype(jnp.bfloat16), 'dp', partner_pairs(self.count, 1...  46.6 us
    ppermute x24, waiting for transfers between devices, step(): lax.ppermute(self.piece, 'dp', partner_pairs(self.count, 1 << bit))  43.9 us
    ppermute x24, starting transfers between devices, step(): lax.ppermute(away.astype(jnp.bfloat16), 'dp', partner_pairs(self.count, 1...  33.9 us
    ppermute x24, starting transfers between devices, step(): lax.ppermute(self.piece, 'dp', partner_pairs(self.count, 1 << bit))  30.6 us
    dot_general x8, matrix products, term(): lax.dot_general(part, right_matrix, (dims, ((), ())), preferred_element_t...  17.3 us
    dynamic_update_slice x30, local copies, waits for them, and re-layouts, put(): lax.dynamic_update_slice(self.held, piece, list(starts) + [zero, zero])  15.8 us
    ppermute x4, waiting for transfers between devices, total_over(): flat = flat + lax.ppermute(flat, 'dp', partner_pairs(data_count, 1 << bit))  11.2 us
    all_gather x4, blocking collectives, spread(): return lax.all_gather(row_block, 'tensor', axis=0, tiled=True)  10.3 us
  transfers between devices with their start and end apart: 57, of which 28 were waited for; matrix products, arithmetic and copies ran while one was open for 21% of the time, Pallas kernels for 4%

commit v1 on v0

--- a/solution.py
+++ b/solution.py
@@ -174,75 +174,68 @@
     return lax.optimization_barrier(values)
 
 
-class Gather:
-    def __init__(self, shard, order, data_rank, data_count, bit_count):
-        self.rows, self.cols = shard.shape
-        self.order, self.count, self.bits = list(order), data_count, bit_count
-        self.mine = [(data_rank >> (bit_count - 1 - place)) & 1 for place in range(bit_count)]
-        self.done = []
-        self.held = jnp.zeros(bit_shape(bit_count) + shard.shape, shard.dtype)
-        self.piece = shard.reshape((1,) * bit_count + shard.shape)
-        self.put(self.piece, self.mine)
-
-    def put(self, piece, starts):
-        zero = jnp.int32(0)
-        self.held = lax.dynamic_update_slice(self.held, piece, list(starts) + [zero, zero])
-
-    def step(self, steps=1):
-        zero = jnp.int32(0)
-        for _ in range(steps):
-            bit = self.order.pop(0)
-            place = self.bits - 1 - bit
-            arrived = lax.ppermute(self.piece, "dp", partner_pairs(self.count, 1 << bit))
-            target = [zero if at in self.done else self.mine[at] for at in range(self.bits)]
-            target[place] = 1 - self.mine[place]
-            self.put(arrived, target)
-            self.done.append(place)
-            if self.order:
-                starts = [zero if at in self.done else self.mine[at] for at in range(self.bits)]
-                sizes = [2 if at in self.done else 1 for at in range(self.bits)]
-                self.piece = lax.dynamic_slice(
-                    self.held, starts + [zero, zero], sizes + [self.rows, self.cols]
-                )
-
-    def whole(self):
-        return self.held.reshape(self.count * self.rows, self.cols)
-
-
-class Scatter:
-    def __init__(self, term, order, data_rank, data_count, bit_count):
-        self.rows, self.cols = term.shape[0] // data_count, term.shape[1]
-        self.order, self.count, self.bits = list(order), data_count, bit_count
-        self.mine = [(data_rank >> (bit_count - 1 - place)) & 1 for place in range(bit_count)]
-        self.held = term.reshape(bit_shape(bit_count) + (self.rows, self.cols))
-
-    def step(self, steps=1):
-        for _ in range(steps):
-            bit = self.order.pop(0)
-            place = self.bits - 1 - bit
-            away = lax.dynamic_slice_in_dim(self.held, 1 - self.mine[place], 1, place)
-            kept = lax.dynamic_slice_in_dim(self.held, self.mine[place], 1, place)
-            arrived = lax.ppermute(
-                away.astype(jnp.bfloat16), "dp", partner_pairs(self.count, 1 << bit)
-            )
-            self.held = kept + arrived.astype(jnp.float32)
-
-    def whole(self):
-        self.step(len(self.order))
-        return self.held.reshape(self.rows, self.cols)
-
-
 def partner_pairs(count, step):
     return [(place, place ^ step) for place in range(count)]
 
 
-def bit_shape(bit_count):
-    return (2,) * bit_count
-
-
-def total_over(flat, data_count, bit_count):
-    for bit in range(bit_count):
-        flat = flat + lax.ppermute(flat, "dp", partner_pairs(data_count, 1 << bit))
+def digits_of(rank, count):
+    sizes, strides, stride = [], [], 1
+    while stride < count:
+        size = min(4, count // stride)
+        sizes.insert(0, size)
+        strides.insert(0, stride)
+        stride *= size
+    return sizes, strides, [(rank // at) % size for at, size in zip(strides, sizes)]
+
+
+def gather_round(held, place, digits, count):
+    sizes, strides, mine = digits
+    zero = jnp.int32(0)
+    shape = held.shape[:place] + (sizes[place],) + held.shape[place:]
+    whole = jnp.zeros(shape, held.dtype)
+    for other in range(sizes[place]):
+        arrived = held
+        if other:
+            arrived = lax.ppermute(held, "dp", partner_pairs(count, other * strides[place]))
+        starts = [zero] * len(shape)
+        starts[place] = mine[place] ^ other
+        whole = lax.dynamic_update_slice(whole, jnp.expand_dims(arrived, place), starts)
+    return whole
+
+
+def gather_rows(shard, digits, count):
+    for place in range(len(digits[0])):
+        shard = gather_round(shard, place, digits, count)
+    return shard.reshape(-1, shard.shape[-1])
+
+
+def split_rows(term, digits, count):
+    return term.reshape(tuple(digits[0]) + (term.shape[0] // count, term.shape[1]))
+
+
+def scatter_round(terms, place, digits, count):
+    sizes, strides, mine = digits
+
+    def block(other):
+        cut = [lax.dynamic_index_in_dim(t, mine[place] ^ other, place, False) for t in terms]
+        return cut
+
+    arrivals = []
+    for other in range(1, sizes[place]):
+        away = jnp.concatenate([cut.astype(jnp.bfloat16) for cut in block(other)], axis=-1)
+        arrivals.append(lax.ppermute(away, "dp", partner_pairs(count, other * strides[place])))
+    total = jnp.concatenate(block(0), axis=-1)
+    for arrived in arrivals:
+        total = total + arrived.astype(jnp.float32)
+    return [total]
+
+
+def total_over(flat, digits, count):
+    for size, stride in zip(digits[0], digits[1]):
+        got = [lax.ppermute(flat, "dp", partner_pairs(count, at * stride)) for at in range(1, size)]
+        flat = flat + got[0]
+        if size == 4:
+            flat = flat + (got[1] + got[2])
     return flat
 
 
@@ -267,35 +260,19 @@
     tensor_rank = lax.axis_index("tensor")
     data_rank = lax.axis_index("dp")
     data_count = lax.axis_size("dp")
-    bit_count = data_count.bit_length() - 1
     head_cols = qkv_weight.shape[2]
     hidden_cols = up_weight.shape[1]
     heads_here = head_cols // HEAD
     block_rows = seq_count * seq_length
-    links = (data_rank, data_count, bit_count)
-    rest = [bit for bit in range(bit_count - 1, 2, -1)]
-    order_up = rest + [2, 1, 0]
-    order_down = rest + [2, 0, 1]
-    order_turn = rest + [1, 0, 2]
-    orders = (order_turn, order_up, order_down)
-
-    qkv_parts = [Gather(qkv_weight[at], orders[at], *links) for at in range(3)]
-    out_part = Gather(out_weight.T, order_turn, *links)
-    up_part = Gather(up_weight, order_up, *links)
-    down_part = Gather(down_weight.T, order_down, *links)
-    later = (out_part, up_part, down_part)
-    early = bit_count - 2
-    for part in qkv_parts:
-        part.step(bit_count - 1)
-    for part in later:
-        part.step(early)
-    tied = tie(*[part.piece for part in qkv_parts], *[part.piece for part in later])
-    for at in range(3):
-        qkv_parts[at].piece, later[at].piece = tied[at], tied[3 + at]
-    for part in qkv_parts:
-        part.step()
-    for part in later:
-        part.step()
+    digits = digits_of(data_rank, data_count)
+    rounds = range(len(digits[0]) - 1, -1, -1)
+
+    first = jnp.concatenate([qkv_weight[0], qkv_weight[1], qkv_weight[2], out_weight.T], axis=1)
+    first_full = gather_rows(first, digits, data_count)
+    up_full = gather_rows(up_weight, digits, data_count)
+    down_full = gather_rows(down_weight.T, digits, data_count)
+    qkv_full = first_full[:, : 3 * head_cols]
+    out_full = first_full[:, 3 * head_cols :]
 
     def spread(row_block):
         return lax.all_gather(row_block, "tensor", axis=0, tiled=True)
@@ -317,23 +294,9 @@
     grad_stream = cotangent.astype(jnp.float32)
     grad_rows = spread(cotangent)
     zeros = jnp.zeros((head_cols,), jnp.float32)
-    biases = (qkv_bias[0], zeros, qkv_bias[1])
-    qkv_full = [part.whole() for part in qkv_parts]
-    stack_rows = jnp.concatenate(
-        [
-            (
-                jnp.dot(hidden_one, qkv_full[at], preferred_element_type=jnp.float32) + biases[at]
-            ).astype(jnp.bfloat16)
-            for at in range(3)
-        ],
-        axis=1,
-    )
-    tied = tie(stack_rows, *[part.piece for part in later])
-    stack_rows = tied[0]
-    for part, piece in zip(later, tied[1:]):
-        part.piece = piece
-        part.step()
-    out_full, up_full, down_full = [part.whole() for part in later]
+    stack_bias = jnp.concatenate([qkv_bias[0], zeros, qkv_bias[1]])
+    stack_rows = jnp.dot(hidden_one, qkv_full, preferred_element_type=jnp.float32) + stack_bias
+    stack_rows = stack_rows.astype(jnp.bfloat16)
     seg_column = segments.reshape(block_rows, 1)
     mixed_rows, log_total = attend(stack_rows, seg_column, segments, head_cols)
     middle = stream + collect(mixed_rows, out_full, turned) + out_biases[0]
@@ -342,14 +305,16 @@
     before = jnp.dot(hidden_two, up_full, preferred_element_type=jnp.float32) + up_bias
     activated = gaussian_unit(before).astype(jnp.bfloat16)
     down_turned = jnp.einsum("rd,rj->dj", grad_rows, activated, preferred_element_type=jnp.float32)
-    down_sum = Scatter(down_turned, order_down[::-1], *links)
-    down_sum.step()
     grad_active = jnp.dot(grad_rows, down_full, preferred_element_type=jnp.float32)
     grad_before = jax.vjp(gaussian_unit, before)[1](grad_active)[0]
     before_low = grad_before.astype(jnp.bfloat16)
     grad_up = jnp.einsum("rd,rj->dj", hidden_two, before_low, preferred_element_type=jnp.float32)
-    up_sum = Scatter(grad_up, order_up[::-1], *links)
-    up_sum.step()
+    wide = scatter_round(
+        [split_rows(grad_up, digits, data_count), split_rows(down_turned, digits, data_count)],
+        rounds[0],
+        digits,
+        data_count,
+    )
     grad_hidden_two = collect(before_low, up_full, turned)
     grad_middle = grad_stream + normalize_back(
         grad_hidden_two, unit_two, inverse_two, norm_gains[1]
@@ -358,24 +323,23 @@
     out_turned = jnp.einsum(
         "rd,rj->dj", middle_rows, mixed_rows, preferred_element_type=jnp.float32
     )
-    out_sum = Scatter(out_turned, order_turn[::-1], *links)
-    out_sum.step()
     grad_mixed = jnp.dot(middle_rows, out_full, preferred_element_type=jnp.float32).astype(
         jnp.bfloat16
     )
-    grad_mixed, down_sum.held = tie(grad_mixed, down_sum.held)
-    down_sum.step()
     result = (middle + collect(activated, down_full, turned) + out_biases[1]).astype(jnp.bfloat16)
     stack_low, bias_sums = attend_back(stack_rows, seg_column, segments, log_total, grad_mixed)
-    stack_low, up_sum.held, out_sum.held = tie(stack_low, up_sum.held, out_sum.held)
-    up_sum.step()
-    out_sum.step()
-    qkv_sums = []
-    for at in range(3):
-        term = dot(hidden_one, stack_low[:, at * head_cols : (at + 1) * head_cols], 0, 0)
-        qkv_sums.append(Scatter(term, orders[at][::-1], *links))
-        qkv_sums[at].step()
-    grad_hidden_one = collect(stack_low, jnp.concatenate(qkv_full, axis=1), turned)
+    stack_low, wide[0] = tie(stack_low, wide[0])
+    grad_qkv = dot(hidden_one, stack_low, 0, 0)
+    slim = scatter_round(
+        [split_rows(grad_qkv, digits, data_count), split_rows(out_turned, digits, data_count)],
+        rounds[0],
+        digits,
+        data_count,
+    )
+    for place in rounds[1:]:
+        wide = scatter_round(wide, place, digits, data_count)
+        slim = scatter_round(slim, place, digits, data_count)
+    grad_hidden_one = collect(stack_low, qkv_full, turned)
     grad_input = grad_middle + normalize_back(grad_hidden_one, unit_one, inverse_one, norm_gains[0])
     vectors = jnp.concatenate(
         [
@@ -395,10 +359,11 @@
             jnp.sum(grad_before, axis=0),
         ]
     )
-    flat = total_over(flat, data_count, bit_count)
-    qkv_summed = jnp.stack([part.whole() for part in qkv_sums])
-    out_summed, down_summed = out_sum.whole().T, down_sum.whole().T
-    up_summed = up_sum.whole()
+    flat = total_over(flat, digits, data_count)
+    qkv_summed = jnp.stack([slim[0][:, at * head_cols : (at + 1) * head_cols] for at in range(3)])
+    out_summed = slim[0][:, 3 * head_cols :].T
+    up_summed = wide[0][:, :hidden_cols]
+    down_summed = wide[0][:, hidden_cols:].T
     vector_total = flat[: 6 * model_width].reshape(6, model_width)
     rest_total = flat[6 * model_width :]
     qkv_bias_grad = rest_total[: 2 * head_cols].reshape(2, head_cols)

time: 289 us -> 285 us (0.986)
  waiting for transfers between devices: 103 us -> 147 us
  local copies, waits for them, and re-layouts: 39.1 us -> 16.9 us
  starting transfers between devices: 72.1 us -> 58.8 us
  matrix products: 35.1 us -> 22.2 us
    ppermute x52 -> x36, waiting for transfers between devices: 102 us -> 144 us  [the longest x18 76.2 us: gather_round(): lax.ppermute(held, 'dp', partner_pairs(count, other * strides[place]))]
    ppermute x52 -> x36, starting transfers between devices: 71.5 us -> 58 us  [the longest x18 27.3 us: gather_round(): lax.ppermute(held, 'dp', partner_pairs(count, other * strides[place]))]
    dynamic_update_slice x30 -> x23, local copies, waits for them, and re-layouts: 15.8 us -> 5.23 us  [gather_round(): lax.dynamic_update_slice(whole, jnp.expand_dims(arrived, place), starts)]
    dynamic_slice x18 -> x0, local copies, waits for them, and re-layouts: 9.95 us -> none  [step(): lax.dynamic_slice(self.held, starts + [zero, zero], sizes + [self.rows, s...]
    dot_general x8, matrix products: 17.3 us -> 9.3 us  [term(): lax.dot_general(part, right_matrix, (dims, ((), ())), preferred_element_t...]
    concatenate x1 -> x8, other arithmetic: 0.1 us -> 5.14 us  [the longest x6 3.66 us: scatter_round(): jnp.concatenate([cut.astype(jnp.bfloat16) for cut in block(other)], axis=-1)]
    another operation x7 -> x6, local copies, waits for them, and re-layouts: 4.95 us -> 0.79 us
  transfers between devices with their start and end apart: 57 -> 41, of which waited for: 28 -> 23; matrix products, arithmetic and copies ran while one was open for 21% -> 11% of each run, Pallas kernels for 4% -> 4%
where the time goes in v1:
time: 285 us; the launch traced here: 284 us
  waiting for transfers between devices  147 us (52%)
  starting transfers between devices  58.8 us (21%)
  matrix products  22.2 us (8%)
  local copies, waits for them, and re-layouts  16.9 us (6%)
  other arithmetic  14.8 us (5%)
  Pallas kernels  12.4 us (4%)
  blocking collectives  10.1 us (4%)
    ppermute x18, waiting for transfers between devices, gather_round(): lax.ppermute(held, 'dp', partner_pairs(count, other * strides[place]))  76.2 us
    ppermute x12, waiting for transfers between devices, scatter_round(): lax.ppermute(away, 'dp', partner_pairs(count, other * strides[place]))  63.6 us
    ppermute x18, starting transfers between devices, gather_round(): lax.ppermute(held, 'dp', partner_pairs(count, other * strides[place]))  27.3 us
    ppermute x12, starting transfers between devices, scatter_round(): lax.ppermute(away, 'dp', partner_pairs(count, other * strides[place]))  22.7 us
    all_gather x4, blocking collectives, spread(): return lax.all_gather(row_block, 'tensor', axis=0, tiled=True)  10.1 us
    dot_general x8, matrix products, term(): lax.dot_general(part, right_matrix, (dims, ((), ())), preferred_element_t...  9.3 us
    ppermute x6, starting transfers between devices, total_over(): lax.ppermute(flat, 'dp', partner_pairs(count, at * stride))  8.01 us
    pallas_call x1, Pallas kernels, attend_back(): pl.pallas_call(attend_back_kernel, grid=(seqs,), in_specs=[row_spec(lengt...  6.81 us
  transfers between devices with their start and end apart: 41, of which 23 were waited for; matrix products, arithmetic and copies ran while one was open for 11% of the time, Pallas kernels for 4%

profile of v1, /device:TPU:0, one launch (start us, length us, event | category | flops | bytes accessed | tf_op | source)
XLA Modules:
  0.0 284.2 jit_solution(11227467652211873316)
XLA Ops:
  1.5 1.5 pad_maximum_fusion.7
  3.0 4.0 %collective-permute-start.1 = (bf16[48,1536]{1,0:T(8,128)(2,1)}, bf16[48,1536]{1,0:T(8,128)(2,1)}, u32[]{:S(2)}, u32[]{:S(2)}) collective-permute-start(bf16[48,1536]{1,0:T(8,128)(2,1)} %pad_maximum_fusion.7), channel_id=1, source_target_pairs={{0,16},{2,18},{4,20},{6,22},{8,24},{10,26},{12,28},{14,30},{16,0},... | collective-permute-start | bytes 442376 | tf_op jit(solution)/shard_map/ppermute | solution.py:199
  7.0 1.6 collective-permute-start
  9.5 2.9 %collective-permute-start.9 = (bf16[48,1536]{1,0:T(8,128)(2,1)}, bf16[48,1536]{1,0:T(8,128)(2,1)}, u32[]{:S(2)}, u32[]{:S(2)}) collective-permute-start(bf16[48,1536]{1,0:T(8,128)(2,1)} %param.20), channel_id=1, source_target_pairs={{0,24},{2,26},{4,28},{6,30},{8,16},{10,18},{12,20},{14,22},{16,8},... | collective-permute-start | bytes 442376 | tf_op jit(solution)/shard_map/ppermute | solution.py:199
  18.5 2.5 all_gather.12
  21.1 2.5 all_gather.14
  25.6 8.5 %collective-permute-done.8 = bf16[48,1536]{1,0:T(8,128)(2,1)S(1)} collective-permute-done((bf16[48,1536]{1,0:T(8,128)(2,1)S(1)}, bf16[48,1536]{1,0:T(8,128)(2,1)S(1)}, u32[]{:S(2)}, u32[]{:S(2)}) %collective-permute-start.8) | collective-permute-done | bytes 147488 | tf_op jit(solution)/shard_map/ppermute | solution.py:199
  34.1 3.3 %collective-permute-start.13 = (bf16[48,1536]{1,0:T(8,128)(2,1)S(1)}, bf16[48,1536]{1,0:T(8,128)(2,1)S(1)}, u32[]{:S(2)}, u32[]{:S(2)}) collective-permute-start(bf16[48,1536]{1,0:T(8,128)(2,1)S(1)} %bitcast.252), channel_id=1, source_target_pairs={{0,8},{2,10},{4,12},{6,14},{8,0},{10,2},{12,4},{14,6},{16,24},{18,... | collective-permute-start | bytes 442376 | tf_op jit(solution)/shard_map/ppermute | solution.py:199
  40.8 2.5 collective-permute-start.12
  47.3 1.5 collective-permute-start.4
  48.9 1.6 collective-permute-start.3
  50.7 30.3 %collective-permute-done.3 = bf16[4,48,1536]{2,1,0:T(8,128)(2,1)S(1)} collective-permute-done((bf16[4,48,1536]{2,1,0:T(8,128)(2,1)S(1)}, bf16[4,48,1536]{2,1,0:T(8,128)(2,1)S(1)}, u32[]{:S(2)}, u32[]{:S(2)}) %collective-permute-start.3) | collective-permute-done | bytes 589856 | tf_op jit(solution)/shard_map/ppermute | solution.py:199
  82.5 1.6 collective-permute-start.18
  84.1 14.1 %collective-permute-done.5 = bf16[4,48,1536]{2,1,0:T(8,128)(2,1)S(1)} collective-permute-done((bf16[4,48,1536]{2,1,0:T(8,128)(2,1)S(1)}, bf16[4,48,1536]{2,1,0:T(8,128)(2,1)S(1)}, u32[]{:S(2)}, u32[]{:S(2)}) %collective-permute-start.5) | collective-permute-done | bytes 589856 | tf_op jit(solution)/shard_map/ppermute | solution.py:199
  98.2 1.5 collective-permute-start.16
  100.9 5.6 %shard_map.203 = (bf16[512,384]{1,0:T(8,128)(2,1)S(1)}, f32[512,6]{1,0:T(8,128)S(1)}) custom-call(bf16[512,1152]{1,0:T(8,128)(2,1)S(1)} %fusion.6.stack_ref, s32[512,1]{1,0:T(8,128)S(1)} %copy.38.seg_column_ref, s32[1,1,512]{2,1,0:T(1,128)S(1)} %bitcast.227), custom_call_target="tpu_custom_call" | custom-call | flops 805306368 | bytes 10000000 | tf_op jit(solution)/shard_map/pallas_call | solution.py:123
  106.5 12.7 %collective-permute-done.16 = bf16[4,48,1536]{2,1,0:T(8,128)(2,1)S(1)} collective-permute-done((bf16[4,48,1536]{2,1,0:T(8,128)(2,1)S(1)}, bf16[4,48,1536]{2,1,0:T(8,128)(2,1)S(1)}, u32[]{:S(2)}, u32[]{:S(2)}) %collective-permute-start.16) | collective-permute-done | bytes 589856 | tf_op jit(solution)/shard_map/ppermute | solution.py:199
  119.2 1.5 collective-permute-start.17
  121.1 10.1 %collective-permute-done.17 = bf16[4,48,1536]{2,1,0:T(8,128)(2,1)S(1)} collective-permute-done((bf16[4,48,1536]{2,1,0:T(8,128)(2,1)S(1)}, bf16[4,48,1536]{2,1,0:T(8,128)(2,1)S(1)}, u32[]{:S(2)}, u32[]{:S(2)}) %collective-permute-start.17) | collective-permute-done | bytes 589856 | tf_op jit(solution)/shard_map/ppermute | solution.py:199
  131.5 2.0 collective-permute-done.6
  134.4 2.5 all_gather.13
  137.0 2.0 multiply_convert_fusion
  139.0 3.2 %fusion.83 = (f32[1536]{0:T(1024)S(1)}, bf16[512,1536]{1,0:T(8,128)(2,1)S(1)}) fusion(f32[512,1536]{1,0:T(8,128)S(1)} %get-tuple-element.78, bf16[512,768]{1,0:T(8,128)(2,1)S(1)} %copy-done.11, bf16[768,1536]{1,0:T(8,128)(2,1)S(1)} %bitcast.243), kind=kOutput, calls=%fused_computation.194 | convolution fusion | flops 1224473088 | bytes 7870464 | tf_op jit(solution)/shard_map/dot_general | solution.py:308
  144.4 1.7 fusion.41
  149.7 2.5 collective-permute-start.23
  155.6 1.5 dynamic-slice_bitcast_fusion
  158.7 2.6 all_gather.15
  161.9 6.8 %shard_map.204 = (bf16[512,1152]{1,0:T(8,128)(2,1)S(1)}, f32[1,8,384]{2,1,0:T(8,128)S(1)}) custom-call(bf16[512,1152]{1,0:T(8,128)(2,1)S(1)} %fusion.6.stack_ref, s32[512,1]{1,0:T(8,128)S(1)} %copy.38.seg_column_ref, s32[1,1,512]{2,1,0:T(1,128)S(1)} %bitcast.228, f32[512,6]{1,0:T(8,128)S(1)} %get-tuple-element.18.log_ref, ...), custom_call_target="tpu_custom_call" | custom-call | flops 2013265920 | bytes 20000000 | tf_op jit(solution)/shard_map/pallas_call | solution.py:147
  168.7 1.9 fusion.89
  170.8 3.1 %fusion.21 = bf16[256,768]{1,0:T(8,128)(2,1)} fusion(f32[256,768]{1,0:T(8,128)S(1)} %get-tuple-element.76, f32[256,768]{1,0:T(8,128)} %collective-permute-done.19, bf16[768,1536]{1,0:T(8,128)(2,1)S(1)} %bitcast.245, bf16[512,1536]{1,0:T(8,128)(2,1)} %copy-done.14, s32[]{:T(128)S(6)} %select_n.108, f32[768]{0:T(1024)S(1)} %get-tuple-element.31), kind=kOutput, calls=%fused_computation.30 | convolution fusion | flops 604766208 | bytes 5114884 | tf_op jit(solution)/shard_map/dot_general | solution.py:283
  173.9 5.9 %collective-permute-done.23 = bf16[4,48,3072]{2,1,0:T(8,128)(2,1)} collective-permute-done((bf16[4,48,3072]{2,1,0:T(8,128)(2,1)}, bf16[4,48,3072]{2,1,0:T(8,128)(2,1)}, u32[]{:S(2)}, u32[]{:S(2)}) %collective-permute-start.23) | collective-permute-done | bytes 1179680 | tf_op jit(solution)/shard_map/ppermute | solution.py:226
  179.8 24.4 %collective-permute-done.22 = bf16[4,48,3072]{2,1,0:T(8,128)(2,1)} collective-permute-done((bf16[4,48,3072]{2,1,0:T(8,128)(2,1)}, bf16[4,48,3072]{2,1,0:T(8,128)(2,1)}, u32[]{:S(2)}, u32[]{:S(2)}) %collective-permute-start.22) | collective-permute-done | bytes 1179680 | tf_op jit(solution)/shard_map/ppermute | solution.py:226
  204.3 2.8 fusion.8
  209.7 2.0 collective-permute-start.38
  211.7 2.5 collective-permute-start.40
  214.9 2.4 collective-permute-start.34
  217.5 1.8 collective-permute-done.38
  220.7 7.6 %collective-permute-done.40 = bf16[48,3072]{1,0:T(8,128)(2,1)S(1)} collective-permute-done((bf16[48,3072]{1,0:T(8,128)(2,1)S(1)}, bf16[48,3072]{1,0:T(8,128)(2,1)S(1)}, u32[]{:S(2)}, u32[]{:S(2)}) %collective-permute-start.40) | collective-permute-done | bytes 294944 | tf_op jit(solution)/shard_map/ppermute | solution.py:226
  228.4 1.5 collective-permute-start.32
  229.9 11.1 %collective-permute-done.39 = bf16[48,3072]{1,0:T(8,128)(2,1)S(1)} collective-permute-done((bf16[48,3072]{1,0:T(8,128)(2,1)S(1)}, bf16[48,3072]{1,0:T(8,128)(2,1)S(1)}, u32[]{:S(2)}, u32[]{:S(2)}) %collective-permute-start.39) | collective-permute-done | bytes 294944 | tf_op jit(solution)/shard_map/ppermute | solution.py:226
  241.1 2.5 collective-permute-done.33
  244.0 5.5 %collective-permute-start.35 = (bf16[48,1536]{1,0:T(8,128)(2,1)S(1)}, bf16[48,1536]{1,0:T(8,128)(2,1)S(1)}, u32[]{:S(2)}, u32[]{:S(2)}) collective-permute-start(bf16[48,1536]{1,0:T(8,128)(2,1)S(1)} %get-tuple-element.55), channel_id=1, source_target_pairs={{0,8},{2,10},{4,12},{6,14},{8,0},{10,2},{12,4},{14,6},{16,24},{18,... | collective-permute-start | bytes 442376 | tf_op jit(solution)/shard_map/ppermute | solution.py:226
  249.5 3.4 %collective-permute-start.37 = (bf16[48,1536]{1,0:T(8,128)(2,1)S(1)}, bf16[48,1536]{1,0:T(8,128)(2,1)S(1)}, u32[]{:S(2)}, u32[]{:S(2)}) collective-permute-start(bf16[48,1536]{1,0:T(8,128)(2,1)S(1)} %get-tuple-element.56), channel_id=1, source_target_pairs={{0,24},{2,26},{4,28},{6,30},{8,16},{10,18},{12,20},{14,22},{16,8},... | collective-permute-start | bytes 442376 | tf_op jit(solution)/shard_map/ppermute | solution.py:226
  253.7 5.3 %collective-permute-done.37 = bf16[48,1536]{1,0:T(8,128)(2,1)S(1)} collective-permute-done((bf16[48,1536]{1,0:T(8,128)(2,1)S(1)}, bf16[48,1536]{1,0:T(8,128)(2,1)S(1)}, u32[]{:S(2)}, u32[]{:S(2)}) %collective-permute-start.37) | collective-permute-done | bytes 147488 | tf_op jit(solution)/shard_map/ppermute | solution.py:226
  259.1 4.7 %collective-permute-done.36 = bf16[48,1536]{1,0:T(8,128)(2,1)S(1)} collective-permute-done((bf16[48,1536]{1,0:T(8,128)(2,1)S(1)}, bf16[48,1536]{1,0:T(8,128)(2,1)S(1)}, u32[]{:S(2)}, u32[]{:S(2)}) %collective-permute-start.36) | collective-permute-done | bytes 147488 | tf_op jit(solution)/shard_map/ppermute | solution.py:226
  267.6 1.6 collective-permute-start.28
  269.2 2.8 collective-permute-start.26
  274.3 2.4 collective-permute-start.31
  (194 shorter events, 52.7 us)
Async XLA Ops:
  0.6 20.4 %copy-start.17 = (bf16[384,48]{0,1:T(8,128)(2,1)S(1)}, bf16[384,48]{0,1:T(8,128)(2,1)}, u32[]{:S(2)}) copy-start(bf16[384,48]{0,1:T(8,128)(2,1)} %param.18) | copy-start | bytes 110596
  1.5 19.6 %copy-start.18 = (bf16[48,1536]{1,0:T(8,128)(2,1)S(1)}, bf16[48,1536]{1,0:T(8,128)(2,1)}, u32[]{:S(2)}) copy-start(bf16[48,1536]{1,0:T(8,128)(2,1)} %param.20) | copy-start | bytes 442372
  3.0 18.2 %copy-start.15 = (bf16[256,768]{1,0:T(8,128)(2,1)S(1)}, bf16[256,768]{1,0:T(8,128)(2,1)}, u32[]{:S(2)}) copy-start(bf16[256,768]{1,0:T(8,128)(2,1)} %param.23) | copy-start | bytes 1179652
  3.0 37.8 %collective-permute-start.1 = (bf16[48,1536]{1,0:T(8,128)(2,1)}, bf16[48,1536]{1,0:T(8,128)(2,1)}, u32[]{:S(2)}, u32[]{:S(2)}) collective-permute-start(bf16[48,1536]{1,0:T(8,128)(2,1)} %pad_maximum_fusion.7), channel_id=1, source_target_pairs={{0,16},{2,18},{4,20},{6,22},{8,24},{10,26},{12,28},{14,30},{16,0},... | collective-permute-start | bytes 442376 | tf_op jit(solution)/shard_map/ppermute | solution.py:199
  7.0 31.6 %collective-permute-start = (bf16[48,1536]{1,0:T(8,128)(2,1)}, bf16[48,1536]{1,0:T(8,128)(2,1)}, u32[]{:S(2)}, u32[]{:S(2)}) collective-permute-start(bf16[48,1536]{1,0:T(8,128)(2,1)} %pad_maximum_fusion.7), channel_id=1, source_target_pairs={{0,8},{2,10},{4,12},{6,14},{8,0},{10,2},{12,4},{14,6},{16,24},{18,... | collective-permute-start | bytes 442376 | tf_op jit(solution)/shard_map/ppermute | solution.py:199
  8.6 35.6 %collective-permute-start.2 = (bf16[48,1536]{1,0:T(8,128)(2,1)}, bf16[48,1536]{1,0:T(8,128)(2,1)}, u32[]{:S(2)}, u32[]{:S(2)}) collective-permute-start(bf16[48,1536]{1,0:T(8,128)(2,1)} %pad_maximum_fusion.7), channel_id=1, source_target_pairs={{0,24},{2,26},{4,28},{6,30},{8,16},{10,18},{12,20},{14,22},{16,8},... | collective-permute-start | bytes 442376 | tf_op jit(solution)/shard_map/ppermute | solution.py:199
  8.6 15.5 %collective-permute-start.7 = (bf16[48,1536]{1,0:T(8,128)(2,1)}, bf16[48,1536]{1,0:T(8,128)(2,1)}, u32[]{:S(2)}, u32[]{:S(2)}) collective-permute-start(bf16[48,1536]{1,0:T(8,128)(2,1)} %param.20), channel_id=1, source_target_pairs={{0,8},{2,10},{4,12},{6,14},{8,0},{10,2},{12,4},{14,6},{16,24},{18,... | collective-permute-start | bytes 442376 | tf_op jit(solution)/shard_map/ppermute | solution.py:199
  9.5 24.6 %collective-permute-start.9 = (bf16[48,1536]{1,0:T(8,128)(2,1)}, bf16[48,1536]{1,0:T(8,128)(2,1)}, u32[]{:S(2)}, u32[]{:S(2)}) collective-permute-start(bf16[48,1536]{1,0:T(8,128)(2,1)} %param.20), channel_id=1, source_target_pairs={{0,24},{2,26},{4,28},{6,30},{8,16},{10,18},{12,20},{14,22},{16,8},... | collective-permute-start | bytes 442376 | tf_op jit(solution)/shard_map/ppermute | solution.py:199
  21.0 78.8 %copy-start.8 = (bf16[512,768]{1,0:T(8,128)(2,1)}, bf16[512,768]{1,0:T(8,128)(2,1)S(1)}, u32[]{:S(2)}) copy-start(bf16[512,768]{1,0:T(8,128)(2,1)S(1)} %all_gather.12) | copy-start | bytes 2359300
  24.1 10.0 %collective-permute-start.8 = (bf16[48,1536]{1,0:T(8,128)(2,1)S(1)}, bf16[48,1536]{1,0:T(8,128)(2,1)S(1)}, u32[]{:S(2)}, u32[]{:S(2)}) collective-permute-start(bf16[48,1536]{1,0:T(8,128)(2,1)S(1)} %copy-done.18), channel_id=1, source_target_pairs={{0,16},{2,18},{4,20},{6,22},{8,24},{10,26},{12,28},{14,30},{16,0},... | collective-permute-start | bytes 442376 | tf_op jit(solution)/shard_map/ppermute | solution.py:199
  34.1 13.2 %collective-permute-start.14 = (bf16[48,1536]{1,0:T(8,128)(2,1)S(1)}, bf16[48,1536]{1,0:T(8,128)(2,1)S(1)}, u32[]{:S(2)}, u32[]{:S(2)}) collective-permute-start(bf16[48,1536]{1,0:T(8,128)(2,1)S(1)} %bitcast.251), channel_id=1, source_target_pairs={{0,16},{2,18},{4,20},{6,22},{8,24},{10,26},{12,28},{14,30},{16,0},... | collective-permute-start | bytes 442376 | tf_op jit(solution)/shard_map/ppermute | solution.py:199
  34.1 11.9 %collective-permute-start.13 = (bf16[48,1536]{1,0:T(8,128)(2,1)S(1)}, bf16[48,1536]{1,0:T(8,128)(2,1)S(1)}, u32[]{:S(2)}, u32[]{:S(2)}) collective-permute-start(bf16[48,1536]{1,0:T(8,128)(2,1)S(1)} %bitcast.252), channel_id=1, source_target_pairs={{0,8},{2,10},{4,12},{6,14},{8,0},{10,2},{12,4},{14,6},{16,24},{18,... | collective-permute-start | bytes 442376 | tf_op jit(solution)/shard_map/ppermute | solution.py:199
  38.6 10.2 %collective-permute-start.15 = (bf16[48,1536]{1,0:T(8,128)(2,1)S(1)}, bf16[48,1536]{1,0:T(8,128)(2,1)S(1)}, u32[]{:S(2)}, u32[]{:S(2)}) collective-permute-start(bf16[48,1536]{1,0:T(8,128)(2,1)S(1)} %bitcast.253), channel_id=1, source_target_pairs={{0,24},{2,26},{4,28},{6,30},{8,16},{10,18},{12,20},{14,22},{16,8},... | collective-permute-start | bytes 442376 | tf_op jit(solution)/shard_map/ppermute | solution.py:199
  40.8 90.7 %collective-permute-start.12 = (bf16[4,48,1536]{2,1,0:T(8,128)(2,1)S(1)}, bf16[4,48,1536]{2,1,0:T(8,128)(2,1)S(1)}, u32[]{:S(2)}, u32[]{:S(2)}) collective-permute-start(bf16[4,48,1536]{2,1,0:T(8,128)(2,1)S(1)} %bitcast_dynamic-update-slice_fusion.16), channel_id=1, source_target_pairs={{0,6},{2,4},{4,2},{6,0},{8,14},{10,12},{12,10},{14,8},{16,22},{18,... | collective-permute-start | bytes 1769480 | tf_op jit(solution)/shard_map/ppermute | solution.py:199
  44.2 87.2 %collective-permute-start.11 = (bf16[4,48,1536]{2,1,0:T(8,128)(2,1)S(1)}, bf16[4,48,1536]{2,1,0:T(8,128)(2,1)S(1)}, u32[]{:S(2)}, u32[]{:S(2)}) collective-permute-start(bf16[4,48,1536]{2,1,0:T(8,128)(2,1)S(1)} %bitcast_dynamic-update-slice_fusion.16), channel_id=1, source_target_pairs={{0,4},{2,6},{4,0},{6,2},{8,12},{10,14},{12,8},{14,10},{16,20},{18,... | collective-permute-start | bytes 1769480 | tf_op jit(solution)/shard_map/ppermute | solution.py:199
  46.0 85.3 %collective-permute-start.10 = (bf16[4,48,1536]{2,1,0:T(8,128)(2,1)S(1)}, bf16[4,48,1536]{2,1,0:T(8,128)(2,1)S(1)}, u32[]{:S(2)}, u32[]{:S(2)}) collective-permute-start(bf16[4,48,1536]{2,1,0:T(8,128)(2,1)S(1)} %bitcast_dynamic-update-slice_fusion.16), channel_id=1, source_target_pairs={{0,2},{2,0},{4,6},{6,4},{8,10},{10,8},{12,14},{14,12},{16,18},{18,... | collective-permute-start | bytes 1769480 | tf_op jit(solution)/shard_map/ppermute | solution.py:199
  47.3 35.2 %collective-permute-start.4 = (bf16[4,48,1536]{2,1,0:T(8,128)(2,1)S(1)}, bf16[4,48,1536]{2,1,0:T(8,128)(2,1)S(1)}, u32[]{:S(2)}, u32[]{:S(2)}) collective-permute-start(bf16[4,48,1536]{2,1,0:T(8,128)(2,1)S(1)} %bitcast_dynamic-update-slice_fusion.20), channel_id=1, source_target_pairs={{0,4},{2,6},{4,0},{6,2},{8,12},{10,14},{12,8},{14,10},{16,20},{18,... | collective-permute-start | bytes 1769480 | tf_op jit(solution)/shard_map/ppermute | solution.py:199
  48.9 32.1 %collective-permute-start.3 = (bf16[4,48,1536]{2,1,0:T(8,128)(2,1)S(1)}, bf16[4,48,1536]{2,1,0:T(8,128)(2,1)S(1)}, u32[]{:S(2)}, u32[]{:S(2)}) collective-permute-start(bf16[4,48,1536]{2,1,0:T(8,128)(2,1)S(1)} %bitcast_dynamic-update-slice_fusion.20), channel_id=1, source_target_pairs={{0,2},{2,0},{4,6},{6,4},{8,10},{10,8},{12,14},{14,12},{16,18},{18,... | collective-permute-start | bytes 1769480 | tf_op jit(solution)/shard_map/ppermute | solution.py:199
  81.0 17.2 %collective-permute-start.5 = (bf16[4,48,1536]{2,1,0:T(8,128)(2,1)S(1)}, bf16[4,48,1536]{2,1,0:T(8,128)(2,1)S(1)}, u32[]{:S(2)}, u32[]{:S(2)}) collective-permute-start(bf16[4,48,1536]{2,1,0:T(8,128)(2,1)S(1)} %bitcast_dynamic-update-slice_fusion.20), channel_id=1, source_target_pairs={{0,6},{2,4},{4,2},{6,0},{8,14},{10,12},{12,10},{14,8},{16,22},{18,... | collective-permute-start | bytes 1769480 | tf_op jit(solution)/shard_map/ppermute | solution.py:199
  82.5 48.8 %collective-permute-start.18 = (bf16[4,48,1536]{2,1,0:T(8,128)(2,1)S(1)}, bf16[4,48,1536]{2,1,0:T(8,128)(2,1)S(1)}, u32[]{:S(2)}, u32[]{:S(2)}) collective-permute-start(bf16[4,48,1536]{2,1,0:T(8,128)(2,1)S(1)} %bitcast_dynamic-update-slice_fusion.13), channel_id=1, source_target_pairs={{0,6},{2,4},{4,2},{6,0},{8,14},{10,12},{12,10},{14,8},{16,22},{18,... | collective-permute-start | bytes 1769480 | tf_op jit(solution)/shard_map/ppermute | solution.py:199
  98.2 21.0 %collective-permute-start.16 = (bf16[4,48,1536]{2,1,0:T(8,128)(2,1)S(1)}, bf16[4,48,1536]{2,1,0:T(8,128)(2,1)S(1)}, u32[]{:S(2)}, u32[]{:S(2)}) collective-permute-start(bf16[4,48,1536]{2,1,0:T(8,128)(2,1)S(1)} %bitcast_dynamic-update-slice_fusion.13), channel_id=1, source_target_pairs={{0,2},{2,0},{4,6},{6,4},{8,10},{10,8},{12,14},{14,12},{16,18},{18,... | collective-permute-start | bytes 1769480 | tf_op jit(solution)/shard_map/ppermute | solution.py:199
  99.7 61.6 %copy-start.4 = (bf16[4,4,48,1536]{3,2,1,0:T(8,128)(2,1)}, bf16[4,4,48,1536]{3,2,1,0:T(8,128)(2,1)S(1)}, u32[]{:S(2)}) copy-start(bf16[4,4,48,1536]{3,2,1,0:T(8,128)(2,1)S(1)} %bitcast_dynamic-update-slice_fusion.11) | copy-start | bytes 7077892
  119.2 12.0 %collective-permute-start.17 = (bf16[4,48,1536]{2,1,0:T(8,128)(2,1)S(1)}, bf16[4,48,1536]{2,1,0:T(8,128)(2,1)S(1)}, u32[]{:S(2)}, u32[]{:S(2)}) collective-permute-start(bf16[4,48,1536]{2,1,0:T(8,128)(2,1)S(1)} %bitcast_dynamic-update-slice_fusion.13), channel_id=1, source_target_pairs={{0,4},{2,6},{4,0},{6,2},{8,12},{10,14},{12,8},{14,10},{16,20},{18,... | collective-permute-start | bytes 1769480 | tf_op jit(solution)/shard_map/ppermute | solution.py:199
  131.2 2.3 collective-permute-start.6
  147.5 23.2 %collective-permute-start.19 = (f32[256,768]{1,0:T(8,128)}, f32[256,768]{1,0:T(8,128)}, u32[]{:S(2)}, u32[]{:S(2)}) collective-permute-start(f32[256,768]{1,0:T(8,128)} %fusion.41), channel_id=1, source_target_pairs={{0,1},{1,0},{2,3},{3,2},{4,5},{5,4},{6,7},{7,6},{8,9},{9,8},{10,11... | collective-permute-start | bytes 2359304 | tf_op jit(solution)/shard_map/ppermute | solution.py:287
  147.7 9.4 %collective-permute-start.20 = (f32[256,768]{1,0:T(8,128)S(1)}, f32[256,768]{1,0:T(8,128)S(1)}, u32[]{:S(2)}, u32[]{:S(2)}) collective-permute-start(f32[256,768]{1,0:T(8,128)S(1)} %fusion.38), channel_id=1, source_target_pairs={{0,1},{1,0},{2,3},{3,2},{4,5},{5,4},{6,7},{7,6},{8,9},{9,8},{10,11... | collective-permute-start | bytes 2359304 | tf_op jit(solution)/shard_map/ppermute | solution.py:287
  149.7 30.1 %collective-permute-start.23 = (bf16[4,48,3072]{2,1,0:T(8,128)(2,1)}, bf16[4,48,3072]{2,1,0:T(8,128)(2,1)}, u32[]{:S(2)}, u32[]{:S(2)}) collective-permute-start(bf16[4,48,3072]{2,1,0:T(8,128)(2,1)} %pad_maximum_fusion.2), channel_id=1, source_target_pairs={{0,6},{2,4},{4,2},{6,0},{8,14},{10,12},{12,10},{14,8},{16,22},{18,... | collective-permute-start | bytes 3538952 | tf_op jit(solution)/shard_map/ppermute | solution.py:226
  153.4 50.8 %collective-permute-start.22 = (bf16[4,48,3072]{2,1,0:T(8,128)(2,1)}, bf16[4,48,3072]{2,1,0:T(8,128)(2,1)}, u32[]{:S(2)}, u32[]{:S(2)}) collective-permute-start(bf16[4,48,3072]{2,1,0:T(8,128)(2,1)} %pad_maximum_fusion.1), channel_id=1, source_target_pairs={{0,4},{2,6},{4,0},{6,2},{8,12},{10,14},{12,8},{14,10},{16,20},{18,... | collective-permute-start | bytes 3538952 | tf_op jit(solution)/shard_map/ppermute | solution.py:226
  155.0 49.3 %collective-permute-start.21 = (bf16[4,48,3072]{2,1,0:T(8,128)(2,1)}, bf16[4,48,3072]{2,1,0:T(8,128)(2,1)}, u32[]{:S(2)}, u32[]{:S(2)}) collective-permute-start(bf16[4,48,3072]{2,1,0:T(8,128)(2,1)} %pad_maximum_fusion), channel_id=1, source_target_pairs={{0,2},{2,0},{4,6},{6,4},{8,10},{10,8},{12,14},{14,12},{16,18},{18,... | collective-permute-start | bytes 3538952 | tf_op jit(solution)/shard_map/ppermute | solution.py:226
  170.7 33.6 %copy-start.6 = (f32[4,48,1536]{2,1,0:T(8,128)S(1)}, f32[4,48,1536]{2,1,0:T(8,128)}, u32[]{:S(2)}) copy-start(f32[4,48,1536]{2,1,0:T(8,128)} %get-tuple-element.82) | copy-start | bytes 3538948
  170.8 33.6 %copy-start.7 = (f32[4,48,1536]{2,1,0:T(8,128)S(1)}, f32[4,48,1536]{2,1,0:T(8,128)}, u32[]{:S(2)}) copy-start(f32[4,48,1536]{2,1,0:T(8,128)} %get-tuple-element.83) | copy-start | bytes 3538948
  209.5 55.7 %collective-permute-start.24 = (f32[256,768]{1,0:T(8,128)S(1)}, f32[256,768]{1,0:T(8,128)S(1)}, u32[]{:S(2)}, u32[]{:S(2)}) collective-permute-start(f32[256,768]{1,0:T(8,128)S(1)} %fusion.9), channel_id=1, source_target_pairs={{0,1},{1,0},{2,3},{3,2},{4,5},{5,4},{6,7},{7,6},{8,9},{9,8},{10,11... | collective-permute-start | bytes 2359304 | tf_op jit(solution)/shard_map/ppermute | solution.py:287
  209.7 9.6 %collective-permute-start.38 = (bf16[48,3072]{1,0:T(8,128)(2,1)S(1)}, bf16[48,3072]{1,0:T(8,128)(2,1)S(1)}, u32[]{:S(2)}, u32[]{:S(2)}) collective-permute-start(bf16[48,3072]{1,0:T(8,128)(2,1)S(1)} %get-tuple-element.52), channel_id=1, source_target_pairs={{0,8},{2,10},{4,12},{6,14},{8,0},{10,2},{12,4},{14,6},{16,24},{18,... | collective-permute-start | bytes 884744 | tf_op jit(solution)/shard_map/ppermute | solution.py:226
  211.7 16.7 %collective-permute-start.40 = (bf16[48,3072]{1,0:T(8,128)(2,1)S(1)}, bf16[48,3072]{1,0:T(8,128)(2,1)S(1)}, u32[]{:S(2)}, u32[]{:S(2)}) collective-permute-start(bf16[48,3072]{1,0:T(8,128)(2,1)S(1)} %get-tuple-element.53), channel_id=1, source_target_pairs={{0,24},{2,26},{4,28},{6,30},{8,16},{10,18},{12,20},{14,22},{16,8},... | collective-permute-start | bytes 884744 | tf_op jit(solution)/shard_map/ppermute | solution.py:226
  214.2 26.8 %collective-permute-start.39 = (bf16[48,3072]{1,0:T(8,128)(2,1)S(1)}, bf16[48,3072]{1,0:T(8,128)(2,1)S(1)}, u32[]{:S(2)}, u32[]{:S(2)}) collective-permute-start(bf16[48,3072]{1,0:T(8,128)(2,1)S(1)} %get-tuple-element.54), channel_id=1, source_target_pairs={{0,16},{2,18},{4,20},{6,22},{8,24},{10,26},{12,28},{14,30},{16,0},... | collective-permute-start | bytes 884744 | tf_op jit(solution)/shard_map/ppermute | solution.py:226
  214.9 26.2 %collective-permute-start.34 = (bf16[4,48,1536]{2,1,0:T(8,128)(2,1)S(1)}, bf16[4,48,1536]{2,1,0:T(8,128)(2,1)S(1)}, u32[]{:S(2)}, u32[]{:S(2)}) collective-permute-start(bf16[4,48,1536]{2,1,0:T(8,128)(2,1)S(1)} %pad_maximum_fusion.5), channel_id=1, source_target_pairs={{0,6},{2,4},{4,2},{6,0},{8,14},{10,12},{12,10},{14,8},{16,22},{18,... | collective-permute-start | bytes 1769480 | tf_op jit(solution)/shard_map/ppermute | solution.py:226
  219.3 24.3 %collective-permute-start.33 = (bf16[4,48,1536]{2,1,0:T(8,128)(2,1)S(1)}, bf16[4,48,1536]{2,1,0:T(8,128)(2,1)S(1)}, u32[]{:S(2)}, u32[]{:S(2)}) collective-permute-start(bf16[4,48,1536]{2,1,0:T(8,128)(2,1)S(1)} %pad_maximum_fusion.4), channel_id=1, source_target_pairs={{0,4},{2,6},{4,0},{6,2},{8,12},{10,14},{12,8},{14,10},{16,20},{18,... | collective-permute-start | bytes 1769480 | tf_op jit(solution)/shard_map/ppermute | solution.py:226
  228.4 15.3 %collective-permute-start.32 = (bf16[4,48,1536]{2,1,0:T(8,128)(2,1)S(1)}, bf16[4,48,1536]{2,1,0:T(8,128)(2,1)S(1)}, u32[]{:S(2)}, u32[]{:S(2)}) collective-permute-start(bf16[4,48,1536]{2,1,0:T(8,128)(2,1)S(1)} %pad_maximum_fusion.3), channel_id=1, source_target_pairs={{0,2},{2,0},{4,6},{6,4},{8,10},{10,8},{12,14},{14,12},{16,18},{18,... | collective-permute-start | bytes 1769480 | tf_op jit(solution)/shard_map/ppermute | solution.py:226
  244.0 9.7 %collective-permute-start.35 = (bf16[48,1536]{1,0:T(8,128)(2,1)S(1)}, bf16[48,1536]{1,0:T(8,128)(2,1)S(1)}, u32[]{:S(2)}, u32[]{:S(2)}) collective-permute-start(bf16[48,1536]{1,0:T(8,128)(2,1)S(1)} %get-tuple-element.55), channel_id=1, source_target_pairs={{0,8},{2,10},{4,12},{6,14},{8,0},{10,2},{12,4},{14,6},{16,24},{18,... | collective-permute-start | bytes 442376 | tf_op jit(solution)/shard_map/ppermute | solution.py:226
  249.5 9.6 %collective-permute-start.37 = (bf16[48,1536]{1,0:T(8,128)(2,1)S(1)}, bf16[48,1536]{1,0:T(8,128)(2,1)S(1)}, u32[]{:S(2)}, u32[]{:S(2)}) collective-permute-start(bf16[48,1536]{1,0:T(8,128)(2,1)S(1)} %get-tuple-element.56), channel_id=1, source_target_pairs={{0,24},{2,26},{4,28},{6,30},{8,16},{10,18},{12,20},{14,22},{16,8},... | collective-permute-start | bytes 442376 | tf_op jit(solution)/shard_map/ppermute | solution.py:226
  252.9 10.9 %collective-permute-start.36 = (bf16[48,1536]{1,0:T(8,128)(2,1)S(1)}, bf16[48,1536]{1,0:T(8,128)(2,1)S(1)}, u32[]{:S(2)}, u32[]{:S(2)}) collective-permute-start(bf16[48,1536]{1,0:T(8,128)(2,1)S(1)} %get-tuple-element.57), channel_id=1, source_target_pairs={{0,16},{2,18},{4,20},{6,22},{8,24},{10,26},{12,28},{14,30},{16,0},... | collective-permute-start | bytes 442376 | tf_op jit(solution)/shard_map/ppermute | solution.py:226
  266.3 1.3 collective-permute-start.25
  267.6 5.7 %collective-permute-start.28 = (f32[6912]{0:T(1024)S(1)}, f32[6912]{0:T(1024)S(1)}, u32[]{:S(2)}, u32[]{:S(2)}) collective-permute-start(f32[6912]{0:T(1024)S(1)} %pad_maximum_fusion.8), channel_id=1, source_target_pairs={{0,24},{2,26},{4,28},{6,30},{8,16},{10,18},{12,20},{14,22},{16,8},... | collective-permute-start | bytes 82952 | tf_op jit(solution)/shard_map/ppermute | solution.py:235
  269.2 4.9 %collective-permute-start.27 = (f32[6912]{0:T(1024)S(1)}, f32[6912]{0:T(1024)S(1)}, u32[]{:S(2)}, u32[]{:S(2)}) collective-permute-start(f32[6912]{0:T(1024)S(1)} %pad_maximum_fusion.8), channel_id=1, source_target_pairs={{0,16},{2,18},{4,20},{6,22},{8,24},{10,26},{12,28},{14,30},{16,0},... | collective-permute-start | bytes 82952 | tf_op jit(solution)/shard_map/ppermute | solution.py:235
  269.2 5.1 %collective-permute-start.26 = (f32[6912]{0:T(1024)S(1)}, f32[6912]{0:T(1024)S(1)}, u32[]{:S(2)}, u32[]{:S(2)}) collective-permute-start(f32[6912]{0:T(1024)S(1)} %pad_maximum_fusion.8), channel_id=1, source_target_pairs={{0,8},{2,10},{4,12},{6,14},{8,0},{10,2},{12,4},{14,6},{16,24},{18,... | collective-permute-start | bytes 82952 | tf_op jit(solution)/shard_map/ppermute | solution.py:235
  274.3 4.9 %collective-permute-start.31 = (f32[6912]{0:T(1024)S(1)}, f32[6912]{0:T(1024)S(1)}, u32[]{:S(2)}, u32[]{:S(2)}) collective-permute-start(f32[6912]{0:T(1024)S(1)} %add_add_fusion.1), channel_id=1, source_target_pairs={{0,6},{2,4},{4,2},{6,0},{8,14},{10,12},{12,10},{14,8},{16,22},{18,... | collective-permute-start | bytes 82952 | tf_op jit(solution)/shard_map/ppermute | solution.py:235
  276.8 3.9 %collective-permute-start.30 = (f32[6912]{0:T(1024)S(1)}, f32[6912]{0:T(1024)S(1)}, u32[]{:S(2)}, u32[]{:S(2)}) collective-permute-start(f32[6912]{0:T(1024)S(1)} %add_add_fusion.1), channel_id=1, source_target_pairs={{0,4},{2,6},{4,0},{6,2},{8,12},{10,14},{12,8},{14,10},{16,20},{18,... | collective-permute-start | bytes 82952 | tf_op jit(solution)/shard_map/ppermute | solution.py:235
  277.4 3.9 %collective-permute-start.29 = (f32[6912]{0:T(1024)S(1)}, f32[6912]{0:T(1024)S(1)}, u32[]{:S(2)}, u32[]{:S(2)}) collective-permute-start(f32[6912]{0:T(1024)S(1)} %add_add_fusion.1), channel_id=1, source_target_pairs={{0,2},{2,0},{4,6},{6,4},{8,10},{10,8},{12,14},{14,12},{16,18},{18,... | collective-permute-start | bytes 82952 | tf_op jit(solution)/shard_map/ppermute | solution.py:235
  (15 other events, 72.0 us)
